TPU v7x, 256 devices: a whole 4x4x8 slice. The times are simulated.
256 devices in a mesh: gz: 8 (over z), gy: 8 (over x, y_hi), gx: 4 (over y_lo, core).
Axes of the slice: x: 4, y: 4 (y_hi: 2, y_lo: 2; y = y_hi * 2 + y_lo), z: 8, core: 2. Of those that a mesh axis runs over, the one named last changes fastest.
Arguments:
- recorded: bfloat16 [6, 3072, 2, 8, 512], P(None, ('gz', 'gy'), None, None, 'gx'), may hold values from 0.19921875 to 2
- tile_place: int32 [6, 3072], replicated, may hold values from 0 to 1023, as said below
- psf: float32 [6, 3, 31], replicated, may hold values from 0.009 to 1
- estimate: float32 [128, 128, 512], P('gz', 'gy', 'gx'), may hold values from 0.34 to 2.81
Outputs:
- restored: float32 [128, 128, 512], P('gz', 'gy', 'gx')
Inputs may be any that keep to these rules, and one draw needn't show every extreme that they name: `tile_place`: tile j belongs to index j // 48 of gz+gy (gz slowest). For each view, the 48 tiles of one index name any block at most 2 times, and one block of each view is named exactly 2 times by the tiles of every index. Positions are below 16.
All inputs are finite; a program needn't handle non-finite values.
Results may differ from a plain program's by a relative error of at most 0.0009.
Values may be sent and summed in bfloat16 or wider, within the bound.
No kernel may reach another device: no remote copies, remote signals or barrier semaphores. Data moves between devices by JAX's collectives and lax.ppermute only.
A program may use at most 128 MiB of HBM per device.

v0:
```python
import jax
import jax.numpy as jnp
from jax import lax
from jax.sharding import PartitionSpec as P

background_level = 0.1
highest = lax.Precision.HIGHEST


def shift(value, axis, step):
    devices = lax.axis_size(axis)
    pairs = [(i, i + step) for i in range(devices) if 0 <= i + step < devices]
    return lax.ppermute(value, axis, pairs)


def taps_table(kernel_set, offset):
    taps = kernel_set.shape[-1]
    table = (offset[:, :, None] == jnp.arange(taps)[None, None, :]).astype(jnp.float32)
    return jnp.einsum("eim,vm->vei", table, kernel_set, precision=highest)


def pack_columns(value, groups):
    rows = value.shape[0] // groups
    return jnp.concatenate([value[g * rows : (g + 1) * rows] for g in range(groups)], axis=1)


def unpack_columns(value, groups):
    width = value.shape[1] // groups
    return jnp.concatenate([value[:, g * width : (g + 1) * width] for g in range(groups)], axis=0)


def route_tiles(recorded, tile_place, positions):
    view_count, slot_count = recorded.shape[:2]
    tile_width = recorded.shape[2] * recorded.shape[3] * recorded.shape[4]
    route_count = lax.axis_size(("gz", "gy"))
    my_index = lax.axis_index(("gz", "gy"))
    capacity = max(2, 2 * slot_count // route_count)
    placed = tile_place.reshape(view_count, route_count, slot_count)
    destination = placed // positions
    position = placed % positions
    matching = destination[..., :, None] == destination[..., None, :]
    earlier = jnp.arange(slot_count)[None, :] < jnp.arange(slot_count)[:, None]
    ranking = jnp.sum(matching & earlier, axis=-1)
    my_dest = lax.dynamic_index_in_dim(destination, my_index, 1, keepdims=False)
    my_rank = lax.dynamic_index_in_dim(ranking, my_index, 1, keepdims=False)
    target = my_dest * capacity + my_rank
    picker = (jnp.arange(route_count * capacity)[None, :, None] == target[:, None, :]).astype(
        jnp.bfloat16
    )
    outgoing = jnp.einsum(
        "vbs,vsk->vbk",
        picker,
        recorded.reshape(view_count, slot_count, tile_width),
        preferred_element_type=jnp.float32,
    ).astype(jnp.bfloat16)
    arrived = lax.all_to_all(outgoing, ("gz", "gy"), split_axis=1, concat_axis=1, tiled=True)
    owned_here = destination == my_index
    at_position = ((position[..., None] == jnp.arange(positions)) & owned_here[..., None]).astype(
        jnp.float32
    )
    at_rank = (ranking[..., None] == jnp.arange(capacity)).astype(jnp.float32)
    placer = (
        jnp.einsum("vrsp,vrsc->vprc", at_position, at_rank)
        .reshape(view_count, positions, route_count * capacity)
        .astype(jnp.bfloat16)
    )
    return jnp.einsum("vpb,vbk->vpk", placer, arrived, preferred_element_type=jnp.float32)


def on_device(recorded, tile_place, psf, estimate):
    view_count = recorded.shape[0]
    tile_depth, tile_rows = recorded.shape[2:4]
    depth, rows, cols = estimate.shape
    per_row = rows // tile_rows
    positions = depth // tile_depth * per_row
    area = depth * rows
    radius = (psf.shape[2] - 1) // 2
    side = 16
    tall, wide = depth + 2 * side, rows + 2 * side
    joined = route_tiles(recorded, tile_place, positions).reshape(view_count, area, cols)

    kernels = psf / jnp.sum(psf, axis=-1, keepdims=True)
    line = jnp.arange(area)
    place, inside = line // (tile_depth * tile_rows), line % (tile_depth * tile_rows)
    line_depth = place // per_row * tile_depth + inside // tile_rows
    line_row = place % per_row * tile_rows + inside % tile_rows
    reach = radius - side
    depth_taps = taps_table(kernels[:, 0], jnp.arange(tall)[:, None] - line_depth[None, :] + reach)
    row_taps = taps_table(kernels[:, 1], jnp.arange(wide)[:, None] - line_row[None, :] + reach)
    depth_taps = depth_taps.transpose(1, 0, 2).reshape(tall, view_count * area)
    row_taps = row_taps.transpose(1, 0, 2).reshape(wide, view_count * area)
    sheet = (depth_taps[:, None, :] * row_taps[None, :, :]).astype(jnp.bfloat16)
    sheet = sheet.reshape(tall * wide, view_count * area)
    column = jnp.concatenate(
        [jnp.arange(cols), jnp.arange(-side, 0), jnp.arange(cols, cols + side)]
    )
    col_taps = taps_table(
        kernels[:, 2], column[:, None] - jnp.arange(cols)[None, :] + radius
    ).astype(jnp.bfloat16)

    own = estimate.astype(jnp.bfloat16)
    own = jnp.concatenate([shift(own, "gy", 1), own, shift(own, "gy", -1)], axis=1)
    own = jnp.concatenate([shift(own, "gz", 1), own, shift(own, "gz", -1)], axis=0)
    own = own.reshape(tall * wide, cols)
    groups = cols // side
    before = unpack_columns(shift(pack_columns(own[:, cols - side :], groups), "gx", 1), groups)
    after = unpack_columns(shift(pack_columns(own[:, :side], groups), "gx", -1), groups)
    field = jnp.concatenate([own, before, after], axis=1)
    swept = lax.dot_general(
        sheet, field, (((0,), (0,)), ((), ())), preferred_element_type=jnp.float32
    )
    swept = swept.astype(jnp.bfloat16).reshape(view_count, area, -1)
    blurred = jnp.einsum("vac,vck->vak", swept, col_taps, preferred_element_type=jnp.float32)
    ratio = (joined / (blurred + background_level)).astype(jnp.bfloat16)

    spread = jnp.einsum("vak,vck->vac", ratio, col_taps, preferred_element_type=jnp.float32)
    spread = spread.astype(jnp.bfloat16).reshape(view_count * area, -1)
    total = jnp.dot(sheet, spread, preferred_element_type=jnp.float32)
    leftward = pack_columns(total[:, cols : cols + side], groups).astype(jnp.bfloat16)
    rightward = pack_columns(total[:, cols + side :], groups).astype(jnp.bfloat16)
    from_right = unpack_columns(shift(leftward, "gx", -1), groups).astype(jnp.float32)
    from_left = unpack_columns(shift(rightward, "gx", 1), groups).astype(jnp.float32)
    edge = jnp.zeros((tall * wide, cols - 2 * side), jnp.float32)
    total = total[:, :cols] + jnp.concatenate([from_left, edge, from_right], axis=1)
    total = total.reshape(tall, wide, cols)
    upper = shift(total[:side].astype(jnp.bfloat16), "gz", -1)
    lower = shift(total[tall - side :].astype(jnp.bfloat16), "gz", 1)
    total = total[side : side + depth] + upper.astype(jnp.float32) + lower.astype(jnp.float32)
    upper = shift(total[:, :side].astype(jnp.bfloat16), "gy", -1)
    lower = shift(total[:, wide - side :].astype(jnp.bfloat16), "gy", 1)
    total = total[:, side : side + rows] + upper.astype(jnp.float32) + lower.astype(jnp.float32)
    return estimate * total / view_count


def solution(mesh):
    placed = (P(None, ("gz", "gy"), None, None, "gx"), P(), P(), P("gz", "gy", "gx"))
    return jax.shard_map(
        on_device, mesh=mesh, in_specs=placed, out_specs=P("gz", "gy", "gx"), check_vma=False
    )
```

profile of v0, /device:TPU:106, one launch (start us, length us, event | category | flops | bytes accessed | tf_op | source)
XLA Modules:
  0.0 188.7 jit_solution(13490179756148840674)
XLA Ops:
  0.0 1.0 convert_element_type.87
  1.0 4.2 %collective-permute-start.1 = (bf16[16,16,128]{2,1,0:T(8,128)(2,1)S(1)}, bf16[16,16,128]{2,1,0:T(8,128)(2,1)S(1)}, u32[]{:S(2)}, u32[]{:S(2)}) collective-permute-start(bf16[16,16,128]{2,1,0:T(8,128)(2,1)S(1)} %convert_element_type.87), channel_id=1, source_target_pairs={{4,0},{8,4},{12,8},{16,12},{20,16},{24,20},{28,24},{5,1},{9,5},{13... | collective-permute-start | bytes 196616 | tf_op jit(solution)/shard_map/ppermute | solution.py:13
  5.2 3.2 %collective-permute-start = (bf16[16,16,128]{2,1,0:T(8,128)(2,1)S(1)}, bf16[16,16,128]{2,1,0:T(8,128)(2,1)S(1)}, u32[]{:S(2)}, u32[]{:S(2)}) collective-permute-start(bf16[16,16,128]{2,1,0:T(8,128)(2,1)S(1)} %convert_element_type.87), channel_id=1, source_target_pairs={{0,4},{4,8},{8,12},{12,16},{16,20},{20,24},{24,28},{1,5},{5,9},{9,... | collective-permute-start | bytes 196616 | tf_op jit(solution)/shard_map/ppermute | solution.py:13
  8.4 1.0 reshape.284
  9.4 0.1 copy.101
  9.5 0.1 broadcast_compare_fusion
  9.7 0.5 reshape.285
  10.2 2.3 %convert_reduce_fusion = s32[6,64,48]{1,2,0:T(8,128)S(1)} fusion(s32[6,64,48]{1,2,0:T(8,128)S(1)} %get-tuple-element.10, pred[48,48]{1,0:T(8,128)(4,1)S(1)} %iota_compare_fusion.9), kind=kLoop, calls=%fused_computation.1 | loop fusion | flops 3520512 | bytes 149760 | tf_op jit(solution)/shard_map/reduce_sum | solution.py:43
  12.5 0.3 add_reduce_fusion
  12.8 1.1 convolution_convert_fusion
  13.9 3.8 %copy.108 = bf16[6,128,2048]{2,0,1:T(8,128)(2,1)} copy(bf16[6,128,2048]{2,1,0:T(8,128)(2,1)S(1)} %convolution_convert_fusion) | data formatting | bytes 6291456 | tf_op jit(solution)/shard_map/convert_element_type | solution.py:55
  17.7 13.7 %all-to-all-start = ((bf16[6,128,2048]{2,0,1:T(8,128)(2,1)}), bf16[6,128,2048]{2,0,1:T(8,128)(2,1)}, u32[]{:S(2)}, u32[]{:S(2)}) async-start(bf16[6,128,2048]{2,0,1:T(8,128)(2,1)} %copy.108), calls=%async_computation | async-start | bytes 8388608 | tf_op jit(solution)/shard_map/all_to_all | solution.py:56
  31.5 0.1 copy.105
  31.9 0.1 copy.107
  32.1 0.1 copy.106
  32.2 0.6 fusion.8
  32.8 1.2 fusion.19
  33.9 0.6 fusion.7
  34.7 5.0 %multiply_convert_fusion = bf16[48,48,1536]{2,1,0:T(8,128)(2,1)} fusion(f32[48,1536]{1,0:T(8,128)S(1)} %bitcast.49, f32[48,1536]{1,0:T(8,128)S(1)} %bitcast.50), kind=kLoop, calls=%fused_computation | loop fusion | flops 7077888 | bytes 7667712 | tf_op jit(solution)/shard_map/convert_element_type | solution.py:92
  39.9 2.4 %collective-permute-start.3 = (bf16[16,48,128]{2,1,0:T(8,128)(2,1)S(1)}, bf16[16,48,128]{2,1,0:T(8,128)(2,1)S(1)}, u32[]{:S(2)}, u32[]{:S(2)}) collective-permute-start(bf16[16,48,128]{2,1,0:T(8,128)(2,1)S(1)} %pad_maximum_fusion.1), channel_id=1, source_target_pairs={{32,0},{64,32},{96,64},{128,96},{160,128},{192,160},{224,192},{33,... | collective-permute-start | bytes 589832 | tf_op jit(solution)/shard_map/ppermute | solution.py:13
  42.3 4.6 %collective-permute-start.2 = (bf16[16,48,128]{2,1,0:T(8,128)(2,1)S(1)}, bf16[16,48,128]{2,1,0:T(8,128)(2,1)S(1)}, u32[]{:S(2)}, u32[]{:S(2)}) collective-permute-start(bf16[16,48,128]{2,1,0:T(8,128)(2,1)S(1)} %pad_maximum_fusion.1), channel_id=1, source_target_pairs={{0,32},{32,64},{64,96},{96,128},{128,160},{160,192},{192,224},{1,3... | collective-permute-start | bytes 589832 | tf_op jit(solution)/shard_map/ppermute | solution.py:13
  47.0 80.4 %collective-permute-done.3 = bf16[16,48,128]{2,1,0:T(8,128)(2,1)S(1)} collective-permute-done((bf16[16,48,128]{2,1,0:T(8,128)(2,1)S(1)}, bf16[16,48,128]{2,1,0:T(8,128)(2,1)S(1)}, u32[]{:S(2)}, u32[]{:S(2)}) %collective-permute-start.3) | collective-permute-done | bytes 196640 | tf_op jit(solution)/shard_map/ppermute | solution.py:13
  127.5 0.2 fusion.48
  127.7 0.2 concatenate.43
  128.0 2.1 %collective-permute-start.4 = (bf16[288,128]{1,0:T(8,128)(2,1)S(1)}, bf16[288,128]{1,0:T(8,128)(2,1)S(1)}, u32[]{:S(2)}, u32[]{:S(2)}) collective-permute-start(bf16[288,128]{1,0:T(8,128)(2,1)S(1)} %concatenate.43), channel_id=1, source_target_pairs={{0,1},{1,2},{2,3},{4,5},{5,6},{6,7},{8,9},{9,10},{10,11},{12,13},{... | collective-permute-start | bytes 221192 | tf_op jit(solution)/shard_map/ppermute | solution.py:13
  130.1 0.9 fusion.5
  131.0 0.2 concatenate.45
  131.2 3.6 %collective-permute-start.5 = (bf16[288,128]{1,0:T(8,128)(2,1)S(1)}, bf16[288,128]{1,0:T(8,128)(2,1)S(1)}, u32[]{:S(2)}, u32[]{:S(2)}) collective-permute-start(bf16[288,128]{1,0:T(8,128)(2,1)S(1)} %concatenate.45), channel_id=1, source_target_pairs={{1,0},{2,1},{3,2},{5,4},{6,5},{7,6},{9,8},{10,9},{11,10},{13,12},{... | collective-permute-start | bytes 221192 | tf_op jit(solution)/shard_map/ppermute | solution.py:13
  134.9 0.1 slice_dynamic-update-slice_fusion.14
  135.0 0.1 slice_dynamic-update-slice_fusion.13
  135.1 0.1 slice_dynamic-update-slice_fusion.12
  135.3 0.1 slice_dynamic-update-slice_fusion.11
  135.4 0.1 slice_dynamic-update-slice_fusion.10
  135.5 0.1 slice_dynamic-update-slice_fusion.9
  135.6 0.1 slice_dynamic-update-slice_fusion.8
  135.7 1.2 collective-permute-done.5
  137.0 0.1 slice_dynamic-update-slice_fusion.5
  137.1 0.1 slice_dynamic-update-slice_fusion.4
  137.2 0.1 slice_dynamic-update-slice_fusion.3
  137.5 0.1 slice_dynamic-update-slice_fusion
  137.6 4.5 %convolution_convert_fusion.1 = bf16[1536,160]{0,1:T(8,128)(2,1)S(1)} fusion(bf16[2304,1536]{1,0:T(8,128)(2,1)} %bitcast.41, bf16[2304,16]{1,0:T(8,128)(2,1)S(1)} %slice_dynamic-update-slice_fusion, bf16[2304,16]{1,0:T(8,128)(2,1)S(1)} %slice_dynamic-update-slice_fusion.8, bf16[2304,128]{1,0:T(8,128)(2,1)S(1)} %bitcast.44), kind=kOutput, calls=%fused_computation.10 | convolution fusion | flops 1134919680 | bytes 8306688 | tf_op jit(solution)/shard_map/dot_general | solution.py:109
  142.1 5.6 %fusion = f32[6,16,2048]{2,1,0:T(8,128)S(1)} fusion(bf16[6,16,128]{1,2,0:T(8,128)(2,1)S(1)} %bitcast.51, bf16[6,128,2048]{2,0,1:T(8,128)(2,1)} %all-to-all-done), kind=kOutput, calls=%fused_computation.3 | convolution fusion | flops 50331648 | bytes 3956736 | tf_op jit(solution)/shard_map/vpb,vbk->vpk/dot_general | solution.py:67
  147.7 0.1 reshape.286
  147.8 0.6 fusion.13
  148.5 5.5 %fusion.52 = (bf16[2304,160]{0,1:T(8,128)(2,1)S(1)}, f32[2304,160]{0,1:T(8,128)S(1)}) fusion(bf16[2304,1536]{1,0:T(8,128)(2,1)} %bitcast.42, bf16[1536,160]{0,1:T(8,128)(2,1)S(1)} %bitcast.45), kind=kOutput, calls=%fused_computation.134 | convolution fusion | flops 1132830720 | bytes 9781248 | tf_op jit(solution)/shard_map/dot_general | solution.py:118
  154.5 1.9 %collective-permute-start.6 = (bf16[288,128]{0,1:T(8,128)(2,1)S(1)}, bf16[288,128]{0,1:T(8,128)(2,1)S(1)}, u32[]{:S(2)}, u32[]{:S(2)}) collective-permute-start(bf16[288,128]{0,1:T(8,128)(2,1)S(1)} %get-tuple-element.11), channel_id=1, source_target_pairs={{0,1},{1,2},{2,3},{4,5},{5,6},{6,7},{8,9},{9,10},{10,11},{12,13},{... | collective-permute-start | bytes 221192 | tf_op jit(solution)/shard_map/ppermute | solution.py:13
  156.5 3.7 %collective-permute-start.7 = (bf16[288,128]{0,1:T(8,128)(2,1)S(1)}, bf16[288,128]{0,1:T(8,128)(2,1)S(1)}, u32[]{:S(2)}, u32[]{:S(2)}) collective-permute-start(bf16[288,128]{0,1:T(8,128)(2,1)S(1)} %get-tuple-element.12), channel_id=1, source_target_pairs={{1,0},{2,1},{3,2},{5,4},{6,5},{7,6},{9,8},{10,9},{11,10},{13,12},{... | collective-permute-start | bytes 221192 | tf_op jit(solution)/shard_map/ppermute | solution.py:13
  160.2 0.3 collective-permute-done.6
  160.5 0.1 concatenate.50
  160.6 1.8 collective-permute-done.7
  162.4 0.1 concatenate.52
  162.6 0.2 fusion.46
  162.8 0.2 copy.115
  163.0 0.2 copy.116
  163.1 2.5 %collective-permute-start.9 = (bf16[16,48,128]{2,1,0:T(8,128)(2,1)S(1)}, bf16[16,48,128]{2,1,0:T(8,128)(2,1)S(1)}, u32[]{:S(2)}, u32[]{:S(2)}) collective-permute-start(bf16[16,48,128]{2,1,0:T(8,128)(2,1)S(1)} %bitcast.53), channel_id=1, source_target_pairs={{0,32},{32,64},{64,96},{96,128},{128,160},{160,192},{192,224},{1,3... | collective-permute-start | bytes 589832 | tf_op jit(solution)/shard_map/ppermute | solution.py:13
  165.7 3.3 %collective-permute-start.8 = (bf16[16,48,128]{2,1,0:T(8,128)(2,1)S(1)}, bf16[16,48,128]{2,1,0:T(8,128)(2,1)S(1)}, u32[]{:S(2)}, u32[]{:S(2)}) collective-permute-start(bf16[16,48,128]{2,1,0:T(8,128)(2,1)S(1)} %bitcast.52), channel_id=1, source_target_pairs={{32,0},{64,32},{96,64},{128,96},{160,128},{192,160},{224,192},{33,... | collective-permute-start | bytes 589832 | tf_op jit(solution)/shard_map/ppermute | solution.py:13
  169.0 0.2 copy.114
  169.2 1.5 collective-permute-done.9
  170.7 3.7 %collective-permute-done.8 = bf16[16,48,128]{2,1,0:T(8,128)(2,1)S(1)} collective-permute-done((bf16[16,48,128]{2,1,0:T(8,128)(2,1)S(1)}, bf16[16,48,128]{2,1,0:T(8,128)(2,1)S(1)}, u32[]{:S(2)}, u32[]{:S(2)}) %collective-permute-start.8) | collective-permute-done | bytes 196640 | tf_op jit(solution)/shard_map/ppermute | solution.py:13
  174.5 4.9 %collective-permute-start.10 = (bf16[16,16,128]{2,1,0:T(8,128)(2,1)S(1)}, bf16[16,16,128]{2,1,0:T(8,128)(2,1)S(1)}, u32[]{:S(2)}, u32[]{:S(2)}) collective-permute-start(bf16[16,16,128]{2,1,0:T(8,128)(2,1)S(1)} %get-tuple-element.45), channel_id=1, source_target_pairs={{4,0},{8,4},{12,8},{16,12},{20,16},{24,20},{28,24},{5,1},{9,5},{13... | collective-permute-start | bytes 196616 | tf_op jit(solution)/shard_map/ppermute | solution.py:13
  179.4 2.5 %collective-permute-start.11 = (bf16[16,16,128]{2,1,0:T(8,128)(2,1)S(1)}, bf16[16,16,128]{2,1,0:T(8,128)(2,1)S(1)}, u32[]{:S(2)}, u32[]{:S(2)}) collective-permute-start(bf16[16,16,128]{2,1,0:T(8,128)(2,1)S(1)} %get-tuple-element.46), channel_id=1, source_target_pairs={{0,4},{4,8},{8,12},{12,16},{16,20},{20,24},{24,28},{1,5},{5,9},{9,... | collective-permute-start | bytes 196616 | tf_op jit(solution)/shard_map/ppermute | solution.py:13
  181.9 1.0 collective-permute-done.10
  182.9 5.1 %collective-permute-done.11 = bf16[16,16,128]{2,1,0:T(8,128)(2,1)S(1)} collective-permute-done((bf16[16,16,128]{2,1,0:T(8,128)(2,1)S(1)}, bf16[16,16,128]{2,1,0:T(8,128)(2,1)S(1)}, u32[]{:S(2)}, u32[]{:S(2)}) %collective-permute-start.11) | collective-permute-done | bytes 65568 | tf_op jit(solution)/shard_map/ppermute | solution.py:13
  188.0 0.7 fusion.35
  (52 shorter events, 1.9 us)
Async XLA Ops:
  0.0 9.6 %copy-start = (bf16[6,48,2,8,128]{4,3,2,1,0:T(8,128)(2,1)S(1)}, bf16[6,48,2,8,128]{4,3,2,1,0:T(8,128)(2,1)}, u32[]{:S(2)}) copy-start(bf16[6,48,2,8,128]{4,3,2,1,0:T(8,128)(2,1)} %param.4) | copy-start | bytes 3538948
  1.0 38.8 %collective-permute-start.1 = (bf16[16,16,128]{2,1,0:T(8,128)(2,1)S(1)}, bf16[16,16,128]{2,1,0:T(8,128)(2,1)S(1)}, u32[]{:S(2)}, u32[]{:S(2)}) collective-permute-start(bf16[16,16,128]{2,1,0:T(8,128)(2,1)S(1)} %convert_element_type.87), channel_id=1, source_target_pairs={{4,0},{8,4},{12,8},{16,12},{20,16},{24,20},{28,24},{5,1},{9,5},{13... | collective-permute-start | bytes 196616 | tf_op jit(solution)/shard_map/ppermute | solution.py:13
  5.2 34.6 %collective-permute-start = (bf16[16,16,128]{2,1,0:T(8,128)(2,1)S(1)}, bf16[16,16,128]{2,1,0:T(8,128)(2,1)S(1)}, u32[]{:S(2)}, u32[]{:S(2)}) collective-permute-start(bf16[16,16,128]{2,1,0:T(8,128)(2,1)S(1)} %convert_element_type.87), channel_id=1, source_target_pairs={{0,4},{4,8},{8,12},{12,16},{16,20},{20,24},{24,28},{1,5},{5,9},{9,... | collective-permute-start | bytes 196616 | tf_op jit(solution)/shard_map/ppermute | solution.py:13
  17.7 13.9 %copy-start.2 = (f32[6,3,31]{2,1,0:T(4,128)S(1)}, f32[6,3,31]{2,1,0:T(4,128)}, u32[]{:S(2)}) copy-start(f32[6,3,31]{2,1,0:T(4,128)} %param.6) | copy-start | bytes 6700
  17.7 124.4 %all-to-all-start = ((bf16[6,128,2048]{2,0,1:T(8,128)(2,1)}), bf16[6,128,2048]{2,0,1:T(8,128)(2,1)}, u32[]{:S(2)}, u32[]{:S(2)}) async-start(bf16[6,128,2048]{2,0,1:T(8,128)(2,1)} %copy.108), calls=%async_computation | async-start | bytes 8388608 | tf_op jit(solution)/shard_map/all_to_all | solution.py:56
  39.9 87.6 %collective-permute-start.3 = (bf16[16,48,128]{2,1,0:T(8,128)(2,1)S(1)}, bf16[16,48,128]{2,1,0:T(8,128)(2,1)S(1)}, u32[]{:S(2)}, u32[]{:S(2)}) collective-permute-start(bf16[16,48,128]{2,1,0:T(8,128)(2,1)S(1)} %pad_maximum_fusion.1), channel_id=1, source_target_pairs={{32,0},{64,32},{96,64},{128,96},{160,128},{192,160},{224,192},{33,... | collective-permute-start | bytes 589832 | tf_op jit(solution)/shard_map/ppermute | solution.py:13
  42.3 85.2 %collective-permute-start.2 = (bf16[16,48,128]{2,1,0:T(8,128)(2,1)S(1)}, bf16[16,48,128]{2,1,0:T(8,128)(2,1)S(1)}, u32[]{:S(2)}, u32[]{:S(2)}) collective-permute-start(bf16[16,48,128]{2,1,0:T(8,128)(2,1)S(1)} %pad_maximum_fusion.1), channel_id=1, source_target_pairs={{0,32},{32,64},{64,96},{96,128},{128,160},{160,192},{192,224},{1,3... | collective-permute-start | bytes 589832 | tf_op jit(solution)/shard_map/ppermute | solution.py:13
  128.0 6.9 %collective-permute-start.4 = (bf16[288,128]{1,0:T(8,128)(2,1)S(1)}, bf16[288,128]{1,0:T(8,128)(2,1)S(1)}, u32[]{:S(2)}, u32[]{:S(2)}) collective-permute-start(bf16[288,128]{1,0:T(8,128)(2,1)S(1)} %concatenate.43), channel_id=1, source_target_pairs={{0,1},{1,2},{2,3},{4,5},{5,6},{6,7},{8,9},{9,10},{10,11},{12,13},{... | collective-permute-start | bytes 221192 | tf_op jit(solution)/shard_map/ppermute | solution.py:13
  131.2 5.6 %collective-permute-start.5 = (bf16[288,128]{1,0:T(8,128)(2,1)S(1)}, bf16[288,128]{1,0:T(8,128)(2,1)S(1)}, u32[]{:S(2)}, u32[]{:S(2)}) collective-permute-start(bf16[288,128]{1,0:T(8,128)(2,1)S(1)} %concatenate.45), channel_id=1, source_target_pairs={{1,0},{2,1},{3,2},{5,4},{6,5},{7,6},{9,8},{10,9},{11,10},{13,12},{... | collective-permute-start | bytes 221192 | tf_op jit(solution)/shard_map/ppermute | solution.py:13
  154.5 6.0 %collective-permute-start.6 = (bf16[288,128]{0,1:T(8,128)(2,1)S(1)}, bf16[288,128]{0,1:T(8,128)(2,1)S(1)}, u32[]{:S(2)}, u32[]{:S(2)}) collective-permute-start(bf16[288,128]{0,1:T(8,128)(2,1)S(1)} %get-tuple-element.11), channel_id=1, source_target_pairs={{0,1},{1,2},{2,3},{4,5},{5,6},{6,7},{8,9},{9,10},{10,11},{12,13},{... | collective-permute-start | bytes 221192 | tf_op jit(solution)/shard_map/ppermute | solution.py:13
  156.5 5.9 %collective-permute-start.7 = (bf16[288,128]{0,1:T(8,128)(2,1)S(1)}, bf16[288,128]{0,1:T(8,128)(2,1)S(1)}, u32[]{:S(2)}, u32[]{:S(2)}) collective-permute-start(bf16[288,128]{0,1:T(8,128)(2,1)S(1)} %get-tuple-element.12), channel_id=1, source_target_pairs={{1,0},{2,1},{3,2},{5,4},{6,5},{7,6},{9,8},{10,9},{11,10},{13,12},{... | collective-permute-start | bytes 221192 | tf_op jit(solution)/shard_map/ppermute | solution.py:13
  162.9 25.0 %copy-start.1 = (f32[16,16,128]{2,1,0:T(8,128)S(1)}, f32[16,16,128]{2,1,0:T(8,128)}, u32[]{:S(2)}) copy-start(f32[16,16,128]{2,1,0:T(8,128)} %param.7) | copy-start | bytes 393220
  163.1 7.6 %collective-permute-start.9 = (bf16[16,48,128]{2,1,0:T(8,128)(2,1)S(1)}, bf16[16,48,128]{2,1,0:T(8,128)(2,1)S(1)}, u32[]{:S(2)}, u32[]{:S(2)}) collective-permute-start(bf16[16,48,128]{2,1,0:T(8,128)(2,1)S(1)} %bitcast.53), channel_id=1, source_target_pairs={{0,32},{32,64},{64,96},{96,128},{128,160},{160,192},{192,224},{1,3... | collective-permute-start | bytes 589832 | tf_op jit(solution)/shard_map/ppermute | solution.py:13
  165.7 8.8 %collective-permute-start.8 = (bf16[16,48,128]{2,1,0:T(8,128)(2,1)S(1)}, bf16[16,48,128]{2,1,0:T(8,128)(2,1)S(1)}, u32[]{:S(2)}, u32[]{:S(2)}) collective-permute-start(bf16[16,48,128]{2,1,0:T(8,128)(2,1)S(1)} %bitcast.52), channel_id=1, source_target_pairs={{32,0},{64,32},{96,64},{128,96},{160,128},{192,160},{224,192},{33,... | collective-permute-start | bytes 589832 | tf_op jit(solution)/shard_map/ppermute | solution.py:13
  174.5 8.4 %collective-permute-start.10 = (bf16[16,16,128]{2,1,0:T(8,128)(2,1)S(1)}, bf16[16,16,128]{2,1,0:T(8,128)(2,1)S(1)}, u32[]{:S(2)}, u32[]{:S(2)}) collective-permute-start(bf16[16,16,128]{2,1,0:T(8,128)(2,1)S(1)} %get-tuple-element.45), channel_id=1, source_target_pairs={{4,0},{8,4},{12,8},{16,12},{20,16},{24,20},{28,24},{5,1},{9,5},{13... | collective-permute-start | bytes 196616 | tf_op jit(solution)/shard_map/ppermute | solution.py:13
  179.4 8.6 %collective-permute-start.11 = (bf16[16,16,128]{2,1,0:T(8,128)(2,1)S(1)}, bf16[16,16,128]{2,1,0:T(8,128)(2,1)S(1)}, u32[]{:S(2)}, u32[]{:S(2)}) collective-permute-start(bf16[16,16,128]{2,1,0:T(8,128)(2,1)S(1)} %get-tuple-element.46), channel_id=1, source_target_pairs={{0,4},{4,8},{8,12},{12,16},{16,20},{20,24},{24,28},{1,5},{5,9},{9,... | collective-permute-start | bytes 196616 | tf_op jit(solution)/shard_map/ppermute | solution.py:13
where the time goes:
time: 191 us; the launch traced here: 189 us
  waiting for transfers between devices  95 us (50%)
  starting transfers between devices  52.6 us (28%)
  matrix products  20.5 us (11%)
  other arithmetic  10.2 us (5%)
  local copies, waits for them, and re-layouts  9.82 us (5%)
    ppermute x12, waiting for transfers between devices, shift(): return lax.ppermute(value, axis, pairs)  95 us
    ppermute x12, starting transfers between devices, shift(): return lax.ppermute(value, axis, pairs)  38.9 us
    all_to_all x1, starting transfers between devices, route_tiles(): lax.all_to_all(outgoing, ('gz', 'gy'), split_axis=1, concat_axis=1, tiled...  13.7 us
    dot_general x1, matrix products, route_tiles(): jnp.einsum('vpb,vbk->vpk', placer, arrived, preferred_element_type=jnp.fl...  5.6 us
    dot_general x1, matrix products, on_device(): total = jnp.dot(sheet, spread, preferred_element_type=jnp.float32)  5.46 us
    convert_element_type x1, other arithmetic, on_device(): sheet = (depth_taps[:, None, :] * row_taps[None, :, :]).astype(jnp.bfloat16)  5.01 us
    dot_general x1, matrix products, on_device(): lax.dot_general(sheet, field, (((0,), (0,)), ((), ())), preferred_element...  4.45 us
  transfers between devices with their start and end apart: 13, of which 8 were waited for; matrix products, arithmetic and copies ran while one was open for 14% of the time, Pallas kernels for 0%

commit v1 on v0

--- a/solution.py
+++ b/solution.py
@@ -1,10 +1,13 @@
 import jax
 import jax.numpy as jnp
 from jax import lax
+from jax.experimental import pallas as pl
+from jax.experimental.pallas import tpu as pltpu
 from jax.sharding import PartitionSpec as P
 
 background_level = 0.1
 highest = lax.Precision.HIGHEST
+capacity = 2
 
 
 def shift(value, axis, step):
@@ -29,42 +32,90 @@
     return jnp.concatenate([value[:, g * width : (g + 1) * width] for g in range(groups)], axis=0)
 
 
-def route_tiles(recorded, tile_place, positions):
-    view_count, slot_count = recorded.shape[:2]
-    tile_width = recorded.shape[2] * recorded.shape[3] * recorded.shape[4]
-    route_count = lax.axis_size(("gz", "gy"))
-    my_index = lax.axis_index(("gz", "gy"))
-    capacity = max(2, 2 * slot_count // route_count)
-    placed = tile_place.reshape(view_count, route_count, slot_count)
+def group_places(tile_place, positions):
+    view_count = tile_place.shape[0]
+    gz_count, gy_count = lax.axis_size("gz"), lax.axis_size("gy")
+    my_gz, my_gy = lax.axis_index("gz"), lax.axis_index("gy")
+    placed = tile_place.reshape(view_count, gz_count, gy_count, -1)
+    placed = lax.dynamic_index_in_dim(placed, my_gz, 1, keepdims=False)
+    slot_count = placed.shape[-1]
     destination = placed // positions
     position = placed % positions
     matching = destination[..., :, None] == destination[..., None, :]
     earlier = jnp.arange(slot_count)[None, :] < jnp.arange(slot_count)[:, None]
     ranking = jnp.sum(matching & earlier, axis=-1)
-    my_dest = lax.dynamic_index_in_dim(destination, my_index, 1, keepdims=False)
-    my_rank = lax.dynamic_index_in_dim(ranking, my_index, 1, keepdims=False)
-    target = my_dest * capacity + my_rank
-    picker = (jnp.arange(route_count * capacity)[None, :, None] == target[:, None, :]).astype(
-        jnp.bfloat16
-    )
-    outgoing = jnp.einsum(
-        "vbs,vsk->vbk",
-        picker,
-        recorded.reshape(view_count, slot_count, tile_width),
-        preferred_element_type=jnp.float32,
-    ).astype(jnp.bfloat16)
-    arrived = lax.all_to_all(outgoing, ("gz", "gy"), split_axis=1, concat_axis=1, tiled=True)
-    owned_here = destination == my_index
-    at_position = ((position[..., None] == jnp.arange(positions)) & owned_here[..., None]).astype(
-        jnp.float32
-    )
-    at_rank = (ranking[..., None] == jnp.arange(capacity)).astype(jnp.float32)
-    placer = (
-        jnp.einsum("vrsp,vrsc->vprc", at_position, at_rank)
-        .reshape(view_count, positions, route_count * capacity)
-        .astype(jnp.bfloat16)
-    )
-    return jnp.einsum("vpb,vbk->vpk", placer, arrived, preferred_element_type=jnp.float32)
+    lane = destination // gy_count * capacity + ranking
+    dest_gy = destination % gy_count
+    lanes = gz_count * capacity
+    own_lane = lax.dynamic_index_in_dim(lane, my_gy, 1, keepdims=False)
+    own_dest = lax.dynamic_index_in_dim(dest_gy, my_gy, 1, keepdims=False)
+    wanted = jnp.arange(gy_count * lanes)[None, :, None]
+    chosen = wanted == (own_dest * lanes + own_lane)[:, None, :]
+    source = jnp.sum(chosen * jnp.arange(slot_count)[None, None, :], axis=-1)
+    here = (dest_gy == my_gy)[:, :, None, :] & (jnp.arange(lanes)[:, None] == lane[:, :, None, :])
+    cell = jnp.sum(here * (position - positions)[:, :, None, :], axis=-1) + positions
+    return source.astype(jnp.int32), cell.astype(jnp.int32)
+
+
+def pack_kernel(source, tiles, outgoing):
+    partners, views, lanes = outgoing.shape[:3]
+    for view in range(views):
+        for partner in range(partners):
+            for lane in range(lanes):
+                index = source[view, partner * lanes + lane]
+                outgoing[partner, view, lane] = tiles[view, index]
+
+
+def join_kernel(cell, arrived, partial, total):
+    partners, views = arrived.shape[:2]
+    blocks, _, positions = partial.shape[:3]
+
+    def one_view(view, carry):
+        for block in range(blocks):
+            total[...] = jnp.zeros_like(total)
+            for partner in range(partners):
+                for rank in range(capacity):
+                    lane = block * capacity + rank
+                    index = cell[view, partner, lane]
+                    total[index] += arrived[partner, view, lane].astype(jnp.float32)
+            partial[block, view] = total[:positions].astype(partial.dtype)
+        return carry
+
+    lax.fori_loop(0, views, one_view, 0)
+
+
+def route_tiles(recorded, tile_place, positions):
+    view_count, slot_count = recorded.shape[:2]
+    height = recorded.shape[2] * recorded.shape[3]
+    cols = recorded.shape[4]
+    gz_count, gy_count = lax.axis_size("gz"), lax.axis_size("gy")
+    source, cell = group_places(tile_place, positions)
+    smem = pl.BlockSpec(memory_space=pltpu.SMEM)
+    vmem = pl.BlockSpec(memory_space=pltpu.VMEM)
+    lanes = gz_count * capacity
+    outgoing = pl.pallas_call(
+        pack_kernel,
+        out_shape=jax.ShapeDtypeStruct((gy_count, view_count, lanes, height, cols), recorded.dtype),
+        in_specs=[smem, vmem],
+        out_specs=vmem,
+        compiler_params=pltpu.CompilerParams(vmem_limit_bytes=32 << 20),
+        name="pack",
+    )(source, recorded.reshape(view_count, slot_count, height, cols))
+    arrived = lax.all_to_all(outgoing, "gy", split_axis=0, concat_axis=0, tiled=True)
+    partial = pl.pallas_call(
+        join_kernel,
+        out_shape=jax.ShapeDtypeStruct(
+            (gz_count, view_count, positions, height, cols), recorded.dtype
+        ),
+        in_specs=[smem, vmem],
+        out_specs=vmem,
+        scratch_shapes=[pltpu.VMEM((positions + 1, height, cols), jnp.float32)],
+        compiler_params=pltpu.CompilerParams(vmem_limit_bytes=32 << 20),
+        name="join",
+    )(cell, arrived)
+    partial = partial.reshape(gz_count, view_count * positions * height, cols)
+    joined = lax.psum_scatter(partial, "gz", scatter_dimension=0, tiled=False)
+    return joined.astype(jnp.float32)
 
 
 def on_device(recorded, tile_place, psf, estimate):
@@ -126,9 +177,9 @@
     upper = shift(total[:side].astype(jnp.bfloat16), "gz", -1)
     lower = shift(total[tall - side :].astype(jnp.bfloat16), "gz", 1)
     total = total[side : side + depth] + upper.astype(jnp.float32) + lower.astype(jnp.float32)
-    upper = shift(total[:, :side].astype(jnp.bfloat16), "gy", -1)
-    lower = shift(total[:, wide - side :].astype(jnp.bfloat16), "gy", 1)
-    total = total[:, side : side + rows] + upper.astype(jnp.float32) + lower.astype(jnp.float32)
+    upper = shift(total[:, :side], "gy", -1)
+    lower = shift(total[:, wide - side :], "gy", 1)
+    total = total[:, side : side + rows] + upper + lower
     return estimate * total / view_count
 
 

time: 191 us -> 172 us (0.901)
  waiting for transfers between devices: 95 us -> 68.2 us
  between operations: 0.59 us -> 13.9 us
  Pallas kernels: 0 us -> 8 us
  starting transfers between devices: 52.6 us -> 45.4 us
  matrix products: 20.5 us -> 13.7 us
  other arithmetic: 10.2 us -> 12.5 us
    ppermute x12, waiting for transfers between devices: 95 us -> 24 us  [shift(): return lax.ppermute(value, axis, pairs)]
    all_to_all x1, waiting for transfers between devices: 0.01 us -> 32.5 us  [route_tiles(): lax.all_to_all(outgoing, 'gy', split_axis=0, concat_axis=0, tiled=True)]
    reduce_scatter x0 -> x1, waiting for transfers between devices: none -> 11.7 us  [route_tiles(): joined = lax.psum_scatter(partial, 'gz', scatter_dimension=0, tiled=False)]
    pallas_call x0 -> x2, Pallas kernels: none -> 8 us  [the longest x1 6.79 us: route_tiles(): pl.pallas_call(join_kernel, out_shape=jax.ShapeDtypeStruct((gz_count, vie...]
    dot_general x3 -> x0, matrix products: 7.85 us -> none  [the longest x1 5.6 us: route_tiles(): jnp.einsum('vpb,vbk->vpk', placer, arrived, preferred_element_type=jnp.fl...]
    all_to_all x1, starting transfers between devices: 13.7 us -> 6.69 us  [route_tiles(): lax.all_to_all(outgoing, 'gy', split_axis=0, concat_axis=0, tiled=True)]
    convert_element_type x1 -> x0, local copies, waits for them, and re-layouts: 3.8 us -> none  [route_tiles(): outgoing = jnp.einsum('vbs,vsk->vbk', picker, recorded.reshape(view_count...]
    unnamed x29 -> x40, local copies, waits for them, and re-layouts: 1.88 us -> 5.56 us
  transfers between devices with their start and end apart: 13 -> 14, of which waited for: 8 -> 11; matrix products, arithmetic and copies ran while one was open for 14% -> 11% of each run, Pallas kernels for 0% -> 4%
where the time goes in v1:
time: 172 us; the launch traced here: 170 us
  waiting for transfers between devices  68.2 us (40%)
  starting transfers between devices  45.4 us (26%)
  between operations  13.9 us (8%)
  matrix products  13.7 us (8%)
  other arithmetic  12.5 us (7%)
  local copies, waits for them, and re-layouts  8.58 us (5%)
  Pallas kernels  8 us (5%)
    ppermute x12, starting transfers between devices, shift(): return lax.ppermute(value, axis, pairs)  38.7 us
    all_to_all x1, waiting for transfers between devices, route_tiles(): lax.all_to_all(outgoing, 'gy', split_axis=0, concat_axis=0, tiled=True)  32.5 us
    ppermute x12, waiting for transfers between devices, shift(): return lax.ppermute(value, axis, pairs)  24 us
    reduce_scatter x1, waiting for transfers between devices, route_tiles(): joined = lax.psum_scatter(partial, 'gz', scatter_dimension=0, tiled=False)  11.7 us
    pallas_call x1, Pallas kernels, route_tiles(): pl.pallas_call(join_kernel, out_shape=jax.ShapeDtypeStruct((gz_count, vie...  6.79 us
    all_to_all x1, starting transfers between devices, route_tiles(): lax.all_to_all(outgoing, 'gy', split_axis=0, concat_axis=0, tiled=True)  6.69 us
    unnamed x40, local copies, waits for them, and re-layouts  5.56 us
    dot_general x1, matrix products, on_device(): total = jnp.dot(sheet, spread, preferred_element_type=jnp.float32)  5.43 us
  transfers between devices with their start and end apart: 14, of which 11 were waited for; matrix products, arithmetic and copies ran while one was open for 11% of the time, Pallas kernels for 4%

profile of v1, /device:TPU:106, one launch (start us, length us, event | category | flops | bytes accessed | tf_op | source)
XLA Modules:
  0.0 170.3 jit_solution(2742491971973014776)
XLA Ops:
  6.5 1.0 reshape.325
  7.6 0.6 broadcast_compare_fusion
  8.2 1.3 convert_reduce_fusion
  9.6 0.1 select_reduce_fusion.1.source
  9.8 1.3 copy-done.1
  11.0 1.2 pack.1
  12.2 1.6 copy-done
  13.9 6.7 %all-to-all-start = ((bf16[8,6,16,16,128]{4,3,2,1,0:T(8,128)(2,1)}), bf16[8,6,16,16,128]{4,3,2,1,0:T(8,128)(2,1)S(1)}, u32[]{:S(2)}, u32[]{:S(2)}) async-start(bf16[8,6,16,16,128]{4,3,2,1,0:T(8,128)(2,1)} %copy-done), calls=%async_computation | async-start | bytes 6291456 | tf_op jit(solution)/shard_map/all_to_all | solution.py:104
  20.6 4.9 %collective-permute-start.1 = (bf16[16,16,128]{2,1,0:T(8,128)(2,1)S(1)}, bf16[16,16,128]{2,1,0:T(8,128)(2,1)}, u32[]{:S(2)}, u32[]{:S(2)}) collective-permute-start(bf16[16,16,128]{2,1,0:T(8,128)(2,1)S(1)} %convert_element_type.71), channel_id=1, source_target_pairs={{4,0},{8,4},{12,8},{16,12},{20,16},{24,20},{28,24},{5,1},{9,5},{13... | collective-permute-start | bytes 196616 | tf_op jit(solution)/shard_map/ppermute | solution.py:16
  25.5 2.5 %collective-permute-start = (bf16[16,16,128]{2,1,0:T(8,128)(2,1)S(1)}, bf16[16,16,128]{2,1,0:T(8,128)(2,1)}, u32[]{:S(2)}, u32[]{:S(2)}) collective-permute-start(bf16[16,16,128]{2,1,0:T(8,128)(2,1)S(1)} %convert_element_type.71), channel_id=1, source_target_pairs={{0,4},{4,8},{8,12},{12,16},{16,20},{20,24},{24,28},{1,5},{5,9},{9,... | collective-permute-start | bytes 196616 | tf_op jit(solution)/shard_map/ppermute | solution.py:16
  28.2 0.6 fusion.2
  29.0 1.6 select_reduce_fusion
  30.5 0.6 subtract_add_fusion.2
  31.2 32.5 %all-to-all-done.arrived = bf16[8,6,16,16,128]{4,3,2,1,0:T(8,128)(2,1)S(1)} async-done(((bf16[8,6,16,16,128]{4,3,2,1,0:T(8,128)(2,1)}), bf16[8,6,16,16,128]{4,3,2,1,0:T(8,128)(2,1)S(1)}, u32[]{:S(2)}, u32[]{:S(2)}) %all-to-all-start) | async-done | bytes 3145760 | tf_op jit(solution)/shard_map/all_to_all | solution.py:104
  63.7 6.8 %join.1 = bf16[8,6,16,16,128]{4,3,2,1,0:T(8,128)(2,1)} custom-call(s32[6,8,16]{2,1,0:T(8,128)S(1)} %broadcast_add_fusion.cell, bf16[8,6,16,16,128]{4,3,2,1,0:T(8,128)(2,1)S(1)} %all-to-all-done.arrived), custom_call_target="tpu_custom_call" | custom-call | tf_op jit(solution)/shard_map/join/pallas_call | solution.py:105
  70.5 0.8 copy-done.4
  71.3 0.6 fusion.1
  72.0 5.0 %multiply_convert_fusion = bf16[48,48,1536]{2,1,0:T(8,128)(2,1)} fusion(f32[48,1536]{1,0:T(8,128)S(1)} %bitcast.76, f32[48,1536]{1,0:T(8,128)S(1)} %bitcast.77), kind=kLoop, calls=%fused_computation | loop fusion | flops 7077888 | bytes 7667712 | tf_op jit(solution)/shard_map/convert_element_type | solution.py:143
  77.1 0.9 pad_maximum_fusion.1
  78.0 2.0 %collective-permute-start.3 = (bf16[16,48,128]{2,1,0:T(8,128)(2,1)S(1)}, bf16[16,48,128]{2,1,0:T(8,128)(2,1)S(1)}, u32[]{:S(2)}, u32[]{:S(2)}) collective-permute-start(bf16[16,48,128]{2,1,0:T(8,128)(2,1)S(1)} %pad_maximum_fusion.1), channel_id=1, source_target_pairs={{32,0},{64,32},{96,64},{128,96},{160,128},{192,160},{224,192},{33,... | collective-permute-start | bytes 589832 | tf_op jit(solution)/shard_map/ppermute | solution.py:16
  80.0 5.1 %collective-permute-start.2 = (bf16[16,48,128]{2,1,0:T(8,128)(2,1)S(1)}, bf16[16,48,128]{2,1,0:T(8,128)(2,1)S(1)}, u32[]{:S(2)}, u32[]{:S(2)}) collective-permute-start(bf16[16,48,128]{2,1,0:T(8,128)(2,1)S(1)} %pad_maximum_fusion.1), channel_id=1, source_target_pairs={{0,32},{32,64},{64,96},{96,128},{128,160},{160,192},{192,224},{1,3... | collective-permute-start | bytes 589832 | tf_op jit(solution)/shard_map/ppermute | solution.py:16
  85.2 1.7 collective-permute-done.3
  86.8 6.6 %collective-permute-done.2 = bf16[16,48,128]{2,1,0:T(8,128)(2,1)S(1)} collective-permute-done((bf16[16,48,128]{2,1,0:T(8,128)(2,1)S(1)}, bf16[16,48,128]{2,1,0:T(8,128)(2,1)S(1)}, u32[]{:S(2)}, u32[]{:S(2)}) %collective-permute-start.2) | collective-permute-done | bytes 196640 | tf_op jit(solution)/shard_map/ppermute | solution.py:16
  93.4 0.9 pad_maximum_fusion
  94.3 0.2 fusion.41
  94.6 0.2 concatenate.43
  94.8 1.9 %collective-permute-start.4 = (bf16[288,128]{1,0:T(8,128)(2,1)S(1)}, bf16[288,128]{1,0:T(8,128)(2,1)S(1)}, u32[]{:S(2)}, u32[]{:S(2)}) collective-permute-start(bf16[288,128]{1,0:T(8,128)(2,1)S(1)} %concatenate.43), channel_id=1, source_target_pairs={{0,1},{1,2},{2,3},{4,5},{5,6},{6,7},{8,9},{9,10},{10,11},{12,13},{... | collective-permute-start | bytes 221192 | tf_op jit(solution)/shard_map/ppermute | solution.py:16
  96.7 0.9 fusion
  97.7 0.2 concatenate.45
  97.9 3.6 %collective-permute-start.5 = (bf16[288,128]{1,0:T(8,128)(2,1)S(1)}, bf16[288,128]{1,0:T(8,128)(2,1)S(1)}, u32[]{:S(2)}, u32[]{:S(2)}) collective-permute-start(bf16[288,128]{1,0:T(8,128)(2,1)S(1)} %concatenate.45), channel_id=1, source_target_pairs={{1,0},{2,1},{3,2},{5,4},{6,5},{7,6},{9,8},{10,9},{11,10},{13,12},{... | collective-permute-start | bytes 221192 | tf_op jit(solution)/shard_map/ppermute | solution.py:16
  101.6 0.1 slice_dynamic-update-slice_fusion.14
  101.7 0.1 slice_dynamic-update-slice_fusion.13
  101.8 0.1 slice_dynamic-update-slice_fusion.12
  101.9 0.1 slice_dynamic-update-slice_fusion.11
  102.0 0.1 slice_dynamic-update-slice_fusion.10
  102.1 0.1 slice_dynamic-update-slice_fusion.9
  102.2 0.1 slice_dynamic-update-slice_fusion.8
  102.4 1.2 collective-permute-done.5
  104.0 0.1 slice_dynamic-update-slice_fusion.2
  104.1 0.1 slice_dynamic-update-slice_fusion.1
  104.2 0.1 slice_dynamic-update-slice_fusion
  104.3 4.5 %convolution_convert_fusion = bf16[1536,160]{0,1:T(8,128)(2,1)S(1)} fusion(bf16[2304,1536]{1,0:T(8,128)(2,1)} %bitcast.68, bf16[2304,16]{1,0:T(8,128)(2,1)S(1)} %slice_dynamic-update-slice_fusion, bf16[2304,16]{1,0:T(8,128)(2,1)S(1)} %slice_dynamic-update-slice_fusion.8, bf16[2304,128]{1,0:T(8,128)(2,1)S(1)} %bitcast.71), kind=kOutput, calls=%fused_computation.3 | convolution fusion | flops 1134919680 | bytes 8306688 | tf_op jit(solution)/shard_map/dot_general | solution.py:160
  108.8 11.7 %reduce-scatter.2.cloned.1.call-done = bf16[1,1536,128]{2,1,0:T(8,128)(2,1)} async-done(((bf16[8,1536,128]{2,1,0:T(8,128)(2,1)}), bf16[1,1536,128]{2,1,0:T(8,128)(2,1)}) %reduce-scatter.2.cloned.1.call-update) | async-done | bytes 393232 | tf_op jit(solution)/shard_map/reduce_scatter | solution.py:117
  120.5 1.6 fusion.6
  122.1 5.4 %fusion.45 = (bf16[2304,160]{0,1:T(8,128)(2,1)S(1)}, f32[2304,160]{0,1:T(8,128)S(1)}) fusion(bf16[2304,1536]{1,0:T(8,128)(2,1)} %bitcast.69, bf16[1536,160]{0,1:T(8,128)(2,1)S(1)} %bitcast.72), kind=kOutput, calls=%fused_computation.140 | convolution fusion | flops 1132830720 | bytes 9781248 | tf_op jit(solution)/shard_map/dot_general | solution.py:169
  128.1 1.9 %collective-permute-start.6 = (bf16[288,128]{0,1:T(8,128)(2,1)S(1)}, bf16[288,128]{0,1:T(8,128)(2,1)S(1)}, u32[]{:S(2)}, u32[]{:S(2)}) collective-permute-start(bf16[288,128]{0,1:T(8,128)(2,1)S(1)} %get-tuple-element.11), channel_id=1, source_target_pairs={{0,1},{1,2},{2,3},{4,5},{5,6},{6,7},{8,9},{9,10},{10,11},{12,13},{... | collective-permute-start | bytes 221192 | tf_op jit(solution)/shard_map/ppermute | solution.py:16
  130.1 3.6 %collective-permute-start.7 = (bf16[288,128]{0,1:T(8,128)(2,1)S(1)}, bf16[288,128]{0,1:T(8,128)(2,1)S(1)}, u32[]{:S(2)}, u32[]{:S(2)}) collective-permute-start(bf16[288,128]{0,1:T(8,128)(2,1)S(1)} %get-tuple-element.12), channel_id=1, source_target_pairs={{1,0},{2,1},{3,2},{5,4},{6,5},{7,6},{9,8},{10,9},{11,10},{13,12},{... | collective-permute-start | bytes 221192 | tf_op jit(solution)/shard_map/ppermute | solution.py:16
  133.8 0.3 collective-permute-done.6
  134.1 0.1 concatenate.50
  134.2 1.8 %collective-permute-done.7 = bf16[288,128]{0,1:T(8,128)(2,1)S(1)} collective-permute-done((bf16[288,128]{0,1:T(8,128)(2,1)S(1)}, bf16[288,128]{0,1:T(8,128)(2,1)S(1)}, u32[]{:S(2)}, u32[]{:S(2)}) %collective-permute-start.7) | collective-permute-done | bytes 73760 | tf_op jit(solution)/shard_map/ppermute | solution.py:16
  136.0 0.1 concatenate.52
  136.1 0.2 fusion.39
  136.3 0.2 copy.70
  136.5 0.2 copy.71
  136.7 3.3 %collective-permute-start.9 = (bf16[16,48,128]{2,1,0:T(8,128)(2,1)S(1)}, bf16[16,48,128]{2,1,0:T(8,128)(2,1)S(1)}, u32[]{:S(2)}, u32[]{:S(2)}) collective-permute-start(bf16[16,48,128]{2,1,0:T(8,128)(2,1)S(1)} %bitcast.79), channel_id=1, source_target_pairs={{0,32},{32,64},{64,96},{96,128},{128,160},{160,192},{192,224},{1,3... | collective-permute-start | bytes 589832 | tf_op jit(solution)/shard_map/ppermute | solution.py:16
  139.9 2.6 %collective-permute-start.8 = (bf16[16,48,128]{2,1,0:T(8,128)(2,1)S(1)}, bf16[16,48,128]{2,1,0:T(8,128)(2,1)S(1)}, u32[]{:S(2)}, u32[]{:S(2)}) collective-permute-start(bf16[16,48,128]{2,1,0:T(8,128)(2,1)S(1)} %bitcast.78), channel_id=1, source_target_pairs={{32,0},{64,32},{96,64},{128,96},{160,128},{192,160},{224,192},{33,... | collective-permute-start | bytes 589832 | tf_op jit(solution)/shard_map/ppermute | solution.py:16
  142.6 0.2 copy.69
  142.7 1.5 collective-permute-done.9
  144.2 4.5 %collective-permute-done.8 = bf16[16,48,128]{2,1,0:T(8,128)(2,1)S(1)} collective-permute-done((bf16[16,48,128]{2,1,0:T(8,128)(2,1)S(1)}, bf16[16,48,128]{2,1,0:T(8,128)(2,1)S(1)}, u32[]{:S(2)}, u32[]{:S(2)}) %collective-permute-start.8) | collective-permute-done | bytes 196640 | tf_op jit(solution)/shard_map/ppermute | solution.py:16
  148.8 4.7 %collective-permute-start.10 = (f32[16,16,128]{2,1,0:T(8,128)S(1)}, f32[16,16,128]{2,1,0:T(8,128)S(1)}, u32[]{:S(2)}, u32[]{:S(2)}) collective-permute-start(f32[16,16,128]{2,1,0:T(8,128)S(1)} %get-tuple-element.45), channel_id=1, source_target_pairs={{4,0},{8,4},{12,8},{16,12},{20,16},{24,20},{28,24},{5,1},{9,5},{13... | collective-permute-start | bytes 393224 | tf_op jit(solution)/shard_map/ppermute | solution.py:16
  153.5 2.7 %collective-permute-start.11 = (f32[16,16,128]{2,1,0:T(8,128)S(1)}, f32[16,16,128]{2,1,0:T(8,128)S(1)}, u32[]{:S(2)}, u32[]{:S(2)}) collective-permute-start(f32[16,16,128]{2,1,0:T(8,128)S(1)} %get-tuple-element.46), channel_id=1, source_target_pairs={{0,4},{4,8},{8,12},{12,16},{16,20},{20,24},{24,28},{1,5},{5,9},{9,... | collective-permute-start | bytes 393224 | tf_op jit(solution)/shard_map/ppermute | solution.py:16
  156.2 2.4 %collective-permute-done.10 = f32[16,16,128]{2,1,0:T(8,128)S(1)} collective-permute-done((f32[16,16,128]{2,1,0:T(8,128)S(1)}, f32[16,16,128]{2,1,0:T(8,128)S(1)}, u32[]{:S(2)}, u32[]{:S(2)}) %collective-permute-start.10) | collective-permute-done | bytes 131104 | tf_op jit(solution)/shard_map/ppermute | solution.py:16
  158.6 4.2 %collective-permute-done.11 = f32[16,16,128]{2,1,0:T(8,128)S(1)} collective-permute-done((f32[16,16,128]{2,1,0:T(8,128)S(1)}, f32[16,16,128]{2,1,0:T(8,128)S(1)}, u32[]{:S(2)}, u32[]{:S(2)}) %collective-permute-start.11) | collective-permute-done | bytes 131104 | tf_op jit(solution)/shard_map/ppermute | solution.py:16
  162.7 0.7 fusion.23
  (60 shorter events, 2.0 us)
Async XLA Ops:
  9.7 1.3 copy-start.1
  12.2 1.6 copy-start
  13.9 6.7 %copy-start.2 = (f32[16,16,128]{2,1,0:T(8,128)S(1)}, f32[16,16,128]{2,1,0:T(8,128)}, u32[]{:S(2)}) copy-start(f32[16,16,128]{2,1,0:T(8,128)} %param.7) | copy-start | bytes 393220
  13.9 14.1 %copy-start.5 = (f32[6,3,31]{2,1,0:T(4,128)S(1)}, f32[6,3,31]{2,1,0:T(4,128)}, u32[]{:S(2)}) copy-start(f32[6,3,31]{2,1,0:T(4,128)} %param.6) | copy-start | bytes 6700
  13.9 49.8 %all-to-all-start = ((bf16[8,6,16,16,128]{4,3,2,1,0:T(8,128)(2,1)}), bf16[8,6,16,16,128]{4,3,2,1,0:T(8,128)(2,1)S(1)}, u32[]{:S(2)}, u32[]{:S(2)}) async-start(bf16[8,6,16,16,128]{4,3,2,1,0:T(8,128)(2,1)} %copy-done), calls=%async_computation | async-start | bytes 6291456 | tf_op jit(solution)/shard_map/all_to_all | solution.py:104
  20.6 99.9 %reduce-scatter.2.cloned.1.call-start = ((), (), s32[]{:S(2)}) async-start(), calls=%async_computation.2 | async-start | bytes 3538944 | tf_op jit(solution)/shard_map/reduce_scatter | solution.py:117
  20.6 56.5 %collective-permute-start.1 = (bf16[16,16,128]{2,1,0:T(8,128)(2,1)S(1)}, bf16[16,16,128]{2,1,0:T(8,128)(2,1)}, u32[]{:S(2)}, u32[]{:S(2)}) collective-permute-start(bf16[16,16,128]{2,1,0:T(8,128)(2,1)S(1)} %convert_element_type.71), channel_id=1, source_target_pairs={{4,0},{8,4},{12,8},{16,12},{20,16},{24,20},{28,24},{5,1},{9,5},{13... | collective-permute-start | bytes 196616 | tf_op jit(solution)/shard_map/ppermute | solution.py:16
  25.5 51.6 %collective-permute-start = (bf16[16,16,128]{2,1,0:T(8,128)(2,1)S(1)}, bf16[16,16,128]{2,1,0:T(8,128)(2,1)}, u32[]{:S(2)}, u32[]{:S(2)}) collective-permute-start(bf16[16,16,128]{2,1,0:T(8,128)(2,1)S(1)} %convert_element_type.71), channel_id=1, source_target_pairs={{0,4},{4,8},{8,12},{12,16},{16,20},{20,24},{24,28},{1,5},{5,9},{9,... | collective-permute-start | bytes 196616 | tf_op jit(solution)/shard_map/ppermute | solution.py:16
  28.2 0.6 copy-start.6
  70.5 0.8 copy-start.4
  70.5 0.8 copy-start.7
  78.0 8.8 %collective-permute-start.3 = (bf16[16,48,128]{2,1,0:T(8,128)(2,1)S(1)}, bf16[16,48,128]{2,1,0:T(8,128)(2,1)S(1)}, u32[]{:S(2)}, u32[]{:S(2)}) collective-permute-start(bf16[16,48,128]{2,1,0:T(8,128)(2,1)S(1)} %pad_maximum_fusion.1), channel_id=1, source_target_pairs={{32,0},{64,32},{96,64},{128,96},{160,128},{192,160},{224,192},{33,... | collective-permute-start | bytes 589832 | tf_op jit(solution)/shard_map/ppermute | solution.py:16
  80.0 13.4 %collective-permute-start.2 = (bf16[16,48,128]{2,1,0:T(8,128)(2,1)S(1)}, bf16[16,48,128]{2,1,0:T(8,128)(2,1)S(1)}, u32[]{:S(2)}, u32[]{:S(2)}) collective-permute-start(bf16[16,48,128]{2,1,0:T(8,128)(2,1)S(1)} %pad_maximum_fusion.1), channel_id=1, source_target_pairs={{0,32},{32,64},{64,96},{96,128},{128,160},{160,192},{192,224},{1,3... | collective-permute-start | bytes 589832 | tf_op jit(solution)/shard_map/ppermute | solution.py:16
  94.8 6.8 %collective-permute-start.4 = (bf16[288,128]{1,0:T(8,128)(2,1)S(1)}, bf16[288,128]{1,0:T(8,128)(2,1)S(1)}, u32[]{:S(2)}, u32[]{:S(2)}) collective-permute-start(bf16[288,128]{1,0:T(8,128)(2,1)S(1)} %concatenate.43), channel_id=1, source_target_pairs={{0,1},{1,2},{2,3},{4,5},{5,6},{6,7},{8,9},{9,10},{10,11},{12,13},{... | collective-permute-start | bytes 221192 | tf_op jit(solution)/shard_map/ppermute | solution.py:16
  97.9 5.6 %collective-permute-start.5 = (bf16[288,128]{1,0:T(8,128)(2,1)S(1)}, bf16[288,128]{1,0:T(8,128)(2,1)S(1)}, u32[]{:S(2)}, u32[]{:S(2)}) collective-permute-start(bf16[288,128]{1,0:T(8,128)(2,1)S(1)} %concatenate.45), channel_id=1, source_target_pairs={{1,0},{2,1},{3,2},{5,4},{6,5},{7,6},{9,8},{10,9},{11,10},{13,12},{... | collective-permute-start | bytes 221192 | tf_op jit(solution)/shard_map/ppermute | solution.py:16
  128.1 5.9 %collective-permute-start.6 = (bf16[288,128]{0,1:T(8,128)(2,1)S(1)}, bf16[288,128]{0,1:T(8,128)(2,1)S(1)}, u32[]{:S(2)}, u32[]{:S(2)}) collective-permute-start(bf16[288,128]{0,1:T(8,128)(2,1)S(1)} %get-tuple-element.11), channel_id=1, source_target_pairs={{0,1},{1,2},{2,3},{4,5},{5,6},{6,7},{8,9},{9,10},{10,11},{12,13},{... | collective-permute-start | bytes 221192 | tf_op jit(solution)/shard_map/ppermute | solution.py:16
  130.1 5.8 %collective-permute-start.7 = (bf16[288,128]{0,1:T(8,128)(2,1)S(1)}, bf16[288,128]{0,1:T(8,128)(2,1)S(1)}, u32[]{:S(2)}, u32[]{:S(2)}) collective-permute-start(bf16[288,128]{0,1:T(8,128)(2,1)S(1)} %get-tuple-element.12), channel_id=1, source_target_pairs={{1,0},{2,1},{3,2},{5,4},{6,5},{7,6},{9,8},{10,9},{11,10},{13,12},{... | collective-permute-start | bytes 221192 | tf_op jit(solution)/shard_map/ppermute | solution.py:16
  136.7 7.6 %collective-permute-start.9 = (bf16[16,48,128]{2,1,0:T(8,128)(2,1)S(1)}, bf16[16,48,128]{2,1,0:T(8,128)(2,1)S(1)}, u32[]{:S(2)}, u32[]{:S(2)}) collective-permute-start(bf16[16,48,128]{2,1,0:T(8,128)(2,1)S(1)} %bitcast.79), channel_id=1, source_target_pairs={{0,32},{32,64},{64,96},{96,128},{128,160},{160,192},{192,224},{1,3... | collective-permute-start | bytes 589832 | tf_op jit(solution)/shard_map/ppermute | solution.py:16
  139.9 8.8 %collective-permute-start.8 = (bf16[16,48,128]{2,1,0:T(8,128)(2,1)S(1)}, bf16[16,48,128]{2,1,0:T(8,128)(2,1)S(1)}, u32[]{:S(2)}, u32[]{:S(2)}) collective-permute-start(bf16[16,48,128]{2,1,0:T(8,128)(2,1)S(1)} %bitcast.78), channel_id=1, source_target_pairs={{32,0},{64,32},{96,64},{128,96},{160,128},{192,160},{224,192},{33,... | collective-permute-start | bytes 589832 | tf_op jit(solution)/shard_map/ppermute | solution.py:16
  142.5 20.2 %copy-start.3 = (f32[16,16,128]{2,1,0:T(8,128)S(1)}, f32[16,16,128]{2,1,0:T(8,128)}, u32[]{:S(2)}) copy-start(f32[16,16,128]{2,1,0:T(8,128)} %param.7) | copy-start | bytes 393220
  148.8 9.8 %collective-permute-start.10 = (f32[16,16,128]{2,1,0:T(8,128)S(1)}, f32[16,16,128]{2,1,0:T(8,128)S(1)}, u32[]{:S(2)}, u32[]{:S(2)}) collective-permute-start(f32[16,16,128]{2,1,0:T(8,128)S(1)} %get-tuple-element.45), channel_id=1, source_target_pairs={{4,0},{8,4},{12,8},{16,12},{20,16},{24,20},{28,24},{5,1},{9,5},{13... | collective-permute-start | bytes 393224 | tf_op jit(solution)/shard_map/ppermute | solution.py:16
  153.5 9.3 %collective-permute-start.11 = (f32[16,16,128]{2,1,0:T(8,128)S(1)}, f32[16,16,128]{2,1,0:T(8,128)S(1)}, u32[]{:S(2)}, u32[]{:S(2)}) collective-permute-start(f32[16,16,128]{2,1,0:T(8,128)S(1)} %get-tuple-element.46), channel_id=1, source_target_pairs={{0,4},{4,8},{8,12},{12,16},{16,20},{20,24},{24,28},{1,5},{5,9},{9,... | collective-permute-start | bytes 393224 | tf_op jit(solution)/shard_map/ppermute | solution.py:16
Sparse Core Ops, SparseCore 0:
  70.7 49.7 reduce-scatter.1

commit v2 on v1

--- a/solution.py
+++ b/solution.py
@@ -44,7 +44,8 @@
     matching = destination[..., :, None] == destination[..., None, :]
     earlier = jnp.arange(slot_count)[None, :] < jnp.arange(slot_count)[:, None]
     ranking = jnp.sum(matching & earlier, axis=-1)
-    lane = destination // gy_count * capacity + ranking
+    ahead = (destination // gy_count - my_gz) % gz_count
+    lane = ahead * capacity + ranking
     dest_gy = destination % gy_count
     lanes = gz_count * capacity
     own_lane = lax.dynamic_index_in_dim(lane, my_gy, 1, keepdims=False)
@@ -84,28 +85,55 @@
     lax.fori_loop(0, views, one_view, 0)
 
 
-def route_tiles(recorded, tile_place, positions):
-    view_count, slot_count = recorded.shape[:2]
-    height = recorded.shape[2] * recorded.shape[3]
-    cols = recorded.shape[4]
+def add_rounded(left, right):
+    return (left.astype(jnp.float32) + right.astype(jnp.float32)).astype(left.dtype)
+
+
+def ring_sum(partial):
+    devices, rows = partial.shape[:2]
+    half, middle = devices // 2, rows // 2
+    up = [(i, (i + 1) % devices) for i in range(devices)]
+    down = [(j, i) for i, j in up]
+    from_below = lax.ppermute(partial[half, :middle], "gz", up)
+    from_above = lax.ppermute(partial[half, middle:], "gz", down)
+    for ahead in range(half - 1, 0, -1):
+        upward, downward = partial[ahead], partial[devices - ahead]
+        if ahead == half - 1:
+            upward = jnp.concatenate([add_rounded(upward[:middle], from_below), upward[middle:]])
+            downward = jnp.concatenate(
+                [downward[:middle], add_rounded(downward[middle:], from_above)]
+            )
+        else:
+            upward = add_rounded(upward, from_below)
+            downward = add_rounded(downward, from_above)
+        from_below = lax.ppermute(upward, "gz", up)
+        from_above = lax.ppermute(downward, "gz", down)
+    return (
+        partial[0].astype(jnp.float32)
+        + from_below.astype(jnp.float32)
+        + from_above.astype(jnp.float32)
+    )
+
+
+def route_tiles(tiles, source, cell, positions):
+    view_count, _, height, cols = tiles.shape
     gz_count, gy_count = lax.axis_size("gz"), lax.axis_size("gy")
-    source, cell = group_places(tile_place, positions)
     smem = pl.BlockSpec(memory_space=pltpu.SMEM)
     vmem = pl.BlockSpec(memory_space=pltpu.VMEM)
     lanes = gz_count * capacity
     outgoing = pl.pallas_call(
         pack_kernel,
-        out_shape=jax.ShapeDtypeStruct((gy_count, view_count, lanes, height, cols), recorded.dtype),
+        out_shape=jax.ShapeDtypeStruct((gy_count, view_count, lanes, height, cols), tiles.dtype),
         in_specs=[smem, vmem],
         out_specs=vmem,
         compiler_params=pltpu.CompilerParams(vmem_limit_bytes=32 << 20),
         name="pack",
-    )(source, recorded.reshape(view_count, slot_count, height, cols))
+    )(source, tiles)
     arrived = lax.all_to_all(outgoing, "gy", split_axis=0, concat_axis=0, tiled=True)
     partial = pl.pallas_call(
         join_kernel,
         out_shape=jax.ShapeDtypeStruct(
-            (gz_count, view_count, positions, height, cols), recorded.dtype
+            (gz_count, view_count, positions, height, cols), tiles.dtype
         ),
         in_specs=[smem, vmem],
         out_specs=vmem,
@@ -113,9 +141,7 @@
         compiler_params=pltpu.CompilerParams(vmem_limit_bytes=32 << 20),
         name="join",
     )(cell, arrived)
-    partial = partial.reshape(gz_count, view_count * positions * height, cols)
-    joined = lax.psum_scatter(partial, "gz", scatter_dimension=0, tiled=False)
-    return joined.astype(jnp.float32)
+    return ring_sum(partial.reshape(gz_count, view_count * positions * height, cols))
 
 
 def on_device(recorded, tile_place, psf, estimate):
@@ -128,7 +154,14 @@
     radius = (psf.shape[2] - 1) // 2
     side = 16
     tall, wide = depth + 2 * side, rows + 2 * side
-    joined = route_tiles(recorded, tile_place, positions).reshape(view_count, area, cols)
+    tiles = recorded.reshape(view_count, -1, tile_depth * tile_rows, cols)
+    source, cell = group_places(tile_place, positions)
+    chunk = view_count // 2
+    joined = [
+        route_tiles(tiles[v : v + chunk], source[v : v + chunk], cell[v : v + chunk], positions)
+        for v in range(0, view_count, chunk)
+    ]
+    joined = jnp.concatenate(joined).reshape(view_count, area, cols)
 
     kernels = psf / jnp.sum(psf, axis=-1, keepdims=True)
     line = jnp.arange(area)

time: 172 us -> 167 us (0.971)
  starting transfers between devices: 45.4 us -> 83.6 us
  waiting for transfers between devices: 68.2 us -> 30.8 us
  between operations: 13.9 us -> 0.78 us
  local copies, waits for them, and re-layouts: 8.58 us -> 13.3 us
    ppermute x0 -> x16, starting transfers between devices: none -> 30.1 us  [the longest x6 21.8 us: ring_sum(): from_below = lax.ppermute(upward, 'gz', up)]
    all_to_all x1 -> x2, waiting for transfers between devices: 32.5 us -> 4.52 us  [route_tiles(): lax.all_to_all(outgoing, 'gy', split_axis=0, concat_axis=0, tiled=True)]
    reduce_scatter x1 -> x0, waiting for transfers between devices: 11.7 us -> none  [route_tiles(): joined = lax.psum_scatter(partial, 'gz', scatter_dimension=0, tiled=False)]
    ppermute x0 -> x16, waiting for transfers between devices: none -> 9.52 us  [the longest x6 6.45 us: ring_sum(): from_above = lax.ppermute(downward, 'gz', down)]
    all_to_all x1 -> x2, starting transfers between devices: 6.69 us -> 14.8 us  [route_tiles(): lax.all_to_all(outgoing, 'gy', split_axis=0, concat_axis=0, tiled=True)]
    ppermute x12, waiting for transfers between devices: 24 us -> 16.8 us  [shift(): return lax.ppermute(value, axis, pairs)]
    pallas_call x1 -> x2, Pallas kernels: 1.21 us -> 4.14 us  [route_tiles(): pl.pallas_call(pack_kernel, out_shape=jax.ShapeDtypeStruct((gy_count, vie...]
    slice x0 -> x9, local copies, waits for them, and re-layouts: none -> 2.02 us  [the longest x1 1.45 us: on_device(): tiles[v:v + chunk]]
  transfers between devices with their start and end apart: 14 -> 30, of which waited for: 11 -> 17; matrix products, arithmetic and copies ran while one was open for 11% -> 18% of each run, Pallas kernels for 4% -> 6%
where the time goes in v2:
time: 167 us; the launch traced here: 164 us
  starting transfers between devices  83.6 us (50%)
  waiting for transfers between devices  30.8 us (18%)
  matrix products  14.5 us (9%)
  local copies, waits for them, and re-layouts  13.3 us (8%)
  other arithmetic  11.6 us (7%)
  Pallas kernels  9.64 us (6%)
    ppermute x12, starting transfers between devices, shift(): return lax.ppermute(value, axis, pairs)  38.7 us
    ppermute x6, starting transfers between devices, ring_sum(): from_below = lax.ppermute(upward, 'gz', up)  21.8 us
    ppermute x12, waiting for transfers between devices, shift(): return lax.ppermute(value, axis, pairs)  16.8 us
    all_to_all x2, starting transfers between devices, route_tiles(): lax.all_to_all(outgoing, 'gy', split_axis=0, concat_axis=0, tiled=True)  14.8 us
    ppermute x2, starting transfers between devices, ring_sum(): from_below = lax.ppermute(partial[half, :middle], 'gz', up)  7.65 us
    ppermute x6, waiting for transfers between devices, ring_sum(): from_above = lax.ppermute(downward, 'gz', down)  6.45 us
    unnamed x34, local copies, waits for them, and re-layouts  6.25 us
    dot_general x1, matrix products, on_device(): lax.dot_general(sheet, field, (((0,), (0,)), ((), ())), preferred_element...  5.62 us
  transfers between devices with their start and end apart: 30, of which 17 were waited for; matrix products, arithmetic and copies ran while one was open for 18% of the time, Pallas kernels for 6%

profile of v2, /device:TPU:106, one launch (start us, length us, event | category | flops | bytes accessed | tf_op | source)
XLA Modules:
  0.0 164.2 jit_solution(6967757086645350206)
XLA Ops:
  0.0 0.9 convert_element_type.270
  0.9 4.2 %collective-permute-start.17 = (bf16[16,16,128]{2,1,0:T(8,128)(2,1)S(1)}, bf16[16,16,128]{2,1,0:T(8,128)(2,1)S(1)}, u32[]{:S(2)}, u32[]{:S(2)}) collective-permute-start(bf16[16,16,128]{2,1,0:T(8,128)(2,1)S(1)} %convert_element_type.270), channel_id=1, source_target_pairs={{4,0},{8,4},{12,8},{16,12},{20,16},{24,20},{28,24},{5,1},{9,5},{13... | collective-permute-start | bytes 196616 | tf_op jit(solution)/shard_map/ppermute | solution.py:16
  5.1 3.2 %collective-permute-start.16 = (bf16[16,16,128]{2,1,0:T(8,128)(2,1)S(1)}, bf16[16,16,128]{2,1,0:T(8,128)(2,1)S(1)}, u32[]{:S(2)}, u32[]{:S(2)}) collective-permute-start(bf16[16,16,128]{2,1,0:T(8,128)(2,1)S(1)} %convert_element_type.270), channel_id=1, source_target_pairs={{0,4},{4,8},{8,12},{12,16},{16,20},{20,24},{24,28},{1,5},{5,9},{9,... | collective-permute-start | bytes 196616 | tf_op jit(solution)/shard_map/ppermute | solution.py:16
  8.3 1.0 reshape.387
  9.4 1.4 convert_reduce_fusion
  11.0 1.4 slice_bitcast_fusion.1
  12.4 2.0 %pack.2 = bf16[8,3,16,16,128]{4,3,2,1,0:T(8,128)(2,1)} custom-call(s32[3,128]{1,0:T(4,128)S(1)} %get-tuple-element.85.source, bf16[3,48,16,128]{3,2,1,0:T(8,128)(2,1)S(1)} %get-tuple-element.29.tiles), custom_call_target="tpu_custom_call" | custom-call | tf_op jit(solution)/shard_map/pack/pallas_call | solution.py:124
  14.4 7.6 %all-to-all-start = ((bf16[8,3,16,16,128]{4,3,2,1,0:T(8,128)(2,1)}), bf16[8,3,16,16,128]{4,3,2,1,0:T(8,128)(2,1)S(1)}, u32[]{:S(2)}, u32[]{:S(2)}) async-start(bf16[8,3,16,16,128]{4,3,2,1,0:T(8,128)(2,1)} %pack.2), calls=%async_computation | async-start | bytes 3145728 | tf_op jit(solution)/shard_map/all_to_all | solution.py:132
  22.5 1.7 %fusion = bf16[6,160,128]{2,0,1:T(8,128)(2,1)} fusion(s32[160,128]{1,0:T(8,128)S(1)} %subtract_add_fusion, f32[6,3,31]{2,0,1:T(8,128)S(1)} %copy_divide_fusion), kind=kOutput, calls=%fused_computation.2 | convolution fusion | flops 46346240 | bytes 331776 | tf_op jit(solution)/shard_map/eim,vm->vei/dot_general | solution.py:22
  24.2 0.6 fusion.2
  24.9 0.6 fusion.1
  25.6 5.0 %multiply_convert_fusion = bf16[48,48,1536]{2,1,0:T(8,128)(2,1)} fusion(f32[48,1536]{1,0:T(8,128)S(1)} %bitcast.123, f32[48,1536]{1,0:T(8,128)S(1)} %bitcast.124), kind=kLoop, calls=%fused_computation | loop fusion | flops 7077888 | bytes 7667712 | tf_op jit(solution)/shard_map/convert_element_type | solution.py:176
  30.6 0.9 select_reduce_fusion
  31.5 2.0 %collective-permute-start.19 = (bf16[16,48,128]{2,1,0:T(8,128)(2,1)S(1)}, bf16[16,48,128]{2,1,0:T(8,128)(2,1)S(1)}, u32[]{:S(2)}, u32[]{:S(2)}) collective-permute-start(bf16[16,48,128]{2,1,0:T(8,128)(2,1)S(1)} %pad_maximum_fusion.6), channel_id=1, source_target_pairs={{32,0},{64,32},{96,64},{128,96},{160,128},{192,160},{224,192},{33,... | collective-permute-start | bytes 589832 | tf_op jit(solution)/shard_map/ppermute | solution.py:16
  33.5 5.0 %collective-permute-start.18 = (bf16[16,48,128]{2,1,0:T(8,128)(2,1)S(1)}, bf16[16,48,128]{2,1,0:T(8,128)(2,1)S(1)}, u32[]{:S(2)}, u32[]{:S(2)}) collective-permute-start(bf16[16,48,128]{2,1,0:T(8,128)(2,1)S(1)} %pad_maximum_fusion.6), channel_id=1, source_target_pairs={{0,32},{32,64},{64,96},{96,128},{128,160},{160,192},{192,224},{1,3... | collective-permute-start | bytes 589832 | tf_op jit(solution)/shard_map/ppermute | solution.py:16
  38.6 1.7 %collective-permute-done.19 = bf16[16,48,128]{2,1,0:T(8,128)(2,1)S(1)} collective-permute-done((bf16[16,48,128]{2,1,0:T(8,128)(2,1)S(1)}, bf16[16,48,128]{2,1,0:T(8,128)(2,1)S(1)}, u32[]{:S(2)}, u32[]{:S(2)}) %collective-permute-start.19) | collective-permute-done | bytes 196640 | tf_op jit(solution)/shard_map/ppermute | solution.py:16
  40.3 1.4 collective-permute-done.18
  41.7 0.9 pad_maximum_fusion.1
  42.6 1.6 fusion.54
  44.4 1.9 %collective-permute-start.20 = (bf16[288,128]{1,0:T(8,128)(2,1)S(1)}, bf16[288,128]{1,0:T(8,128)(2,1)S(1)}, u32[]{:S(2)}, u32[]{:S(2)}) collective-permute-start(bf16[288,128]{1,0:T(8,128)(2,1)S(1)} %concatenate.63), channel_id=1, source_target_pairs={{0,1},{1,2},{2,3},{4,5},{5,6},{6,7},{8,9},{9,10},{10,11},{12,13},{... | collective-permute-start | bytes 221192 | tf_op jit(solution)/shard_map/ppermute | solution.py:16
  46.4 2.1 %pack.3 = bf16[8,3,16,16,128]{4,3,2,1,0:T(8,128)(2,1)} custom-call(s32[3,128]{1,0:T(4,128)S(1)} %get-tuple-element.86.source, bf16[3,48,16,128]{3,2,1,0:T(8,128)(2,1)S(1)} %get-tuple-element.30.tiles), custom_call_target="tpu_custom_call" | custom-call | tf_op jit(solution)/shard_map/pack/pallas_call | solution.py:124
  48.7 3.6 %collective-permute-start.21 = (bf16[288,128]{1,0:T(8,128)(2,1)S(1)}, bf16[288,128]{1,0:T(8,128)(2,1)S(1)}, u32[]{:S(2)}, u32[]{:S(2)}) collective-permute-start(bf16[288,128]{1,0:T(8,128)(2,1)S(1)} %concatenate.65), channel_id=1, source_target_pairs={{1,0},{2,1},{3,2},{5,4},{6,5},{7,6},{9,8},{10,9},{11,10},{13,12},{... | collective-permute-start | bytes 221192 | tf_op jit(solution)/shard_map/ppermute | solution.py:16
  53.2 1.2 collective-permute-done.21
  54.3 0.6 slice_dynamic-update-slice_fusion.7
  55.0 0.7 slice_dynamic-update-slice_fusion.6
  55.7 0.7 slice_dynamic-update-slice_fusion.5
  56.4 0.7 slice_dynamic-update-slice_fusion.4
  57.1 0.7 slice_dynamic-update-slice_fusion.3
  57.9 0.7 slice_dynamic-update-slice_fusion.2
  58.6 7.2 %all-to-all-start.1 = ((bf16[8,3,16,16,128]{4,3,2,1,0:T(8,128)(2,1)}), bf16[8,3,16,16,128]{4,3,2,1,0:T(8,128)(2,1)S(1)}, u32[]{:S(2)}, u32[]{:S(2)}) async-start(bf16[8,3,16,16,128]{4,3,2,1,0:T(8,128)(2,1)} %pack.3), calls=%async_computation.1 | async-start | bytes 3145728 | tf_op jit(solution)/shard_map/all_to_all | solution.py:132
  65.8 0.7 slice_dynamic-update-slice_fusion.1
  66.5 0.7 slice_dynamic-update-slice_fusion
  67.2 5.6 %convolution_convert_fusion = bf16[1536,160]{0,1:T(8,128)(2,1)} fusion(bf16[2304,1536]{1,0:T(8,128)(2,1)} %bitcast.117, bf16[2304,16]{1,0:T(8,128)(2,1)} %slice_dynamic-update-slice_fusion, bf16[2304,16]{1,0:T(8,128)(2,1)} %copy-done.2, bf16[2304,128]{1,0:T(8,128)(2,1)} %bitcast.31), kind=kOutput, calls=%fused_computation.3 | convolution fusion | flops 1134919680 | bytes 8306688 | tf_op jit(solution)/shard_map/dot_general | solution.py:193
  72.8 2.8 %join.2 = bf16[8,3,16,16,128]{4,3,2,1,0:T(8,128)(2,1)S(1)} custom-call(s32[3,8,16]{2,1,0:T(8,128)S(1)} %get-tuple-element.83.cell, bf16[8,3,16,16,128]{4,3,2,1,0:T(8,128)(2,1)S(1)} %all-to-all-done.arrived), custom_call_target="tpu_custom_call" | custom-call | tf_op jit(solution)/shard_map/join/pallas_call | solution.py:133
  75.7 3.8 %collective-permute-start = (bf16[384,128]{1,0:T(8,128)(2,1)S(1)}, bf16[384,128]{1,0:T(8,128)(2,1)S(1)}, u32[]{:S(2)}, u32[]{:S(2)}) collective-permute-start(bf16[384,128]{1,0:T(8,128)(2,1)S(1)} %get-tuple-element.18), channel_id=1, source_target_pairs={{0,32},{32,64},{64,96},{96,128},{128,160},{160,192},{192,224},{224... | collective-permute-start | bytes 294920 | tf_op jit(solution)/shard_map/ppermute | solution.py:97
  79.7 4.5 %all-to-all-done.1.arrived = bf16[8,3,16,16,128]{4,3,2,1,0:T(8,128)(2,1)S(1)} async-done(((bf16[8,3,16,16,128]{4,3,2,1,0:T(8,128)(2,1)}), bf16[8,3,16,16,128]{4,3,2,1,0:T(8,128)(2,1)S(1)}, u32[]{:S(2)}, u32[]{:S(2)}) %all-to-all-start.1) | async-done | bytes 1572896 | tf_op jit(solution)/shard_map/all_to_all | solution.py:132
  84.2 2.7 %join.3 = bf16[8,3,16,16,128]{4,3,2,1,0:T(8,128)(2,1)S(1)} custom-call(s32[3,8,16]{2,1,0:T(8,128)S(1)} %get-tuple-element.84.cell, bf16[8,3,16,16,128]{4,3,2,1,0:T(8,128)(2,1)S(1)} %all-to-all-done.1.arrived), custom_call_target="tpu_custom_call" | custom-call | tf_op jit(solution)/shard_map/join/pallas_call | solution.py:133
  87.3 3.9 %collective-permute-start.8 = (bf16[384,128]{1,0:T(8,128)(2,1)S(1)}, bf16[384,128]{1,0:T(8,128)(2,1)S(1)}, u32[]{:S(2)}, u32[]{:S(2)}) collective-permute-start(bf16[384,128]{1,0:T(8,128)(2,1)S(1)} %get-tuple-element.27), channel_id=1, source_target_pairs={{0,32},{32,64},{64,96},{96,128},{128,160},{160,192},{192,224},{224... | collective-permute-start | bytes 294920 | tf_op jit(solution)/shard_map/ppermute | solution.py:97
  91.3 3.3 %collective-permute-start.1 = (bf16[768,128]{1,0:T(8,128)(2,1)S(1)}, bf16[768,128]{1,0:T(8,128)(2,1)S(1)}, u32[]{:S(2)}, u32[]{:S(2)}) collective-permute-start(bf16[768,128]{1,0:T(8,128)(2,1)S(1)} %pad_maximum_fusion.2), channel_id=1, source_target_pairs={{0,32},{32,64},{64,96},{96,128},{128,160},{160,192},{192,224},{224... | collective-permute-start | bytes 589832 | tf_op jit(solution)/shard_map/ppermute | solution.py:109
  94.8 3.4 %collective-permute-start.9 = (bf16[768,128]{1,0:T(8,128)(2,1)S(1)}, bf16[768,128]{1,0:T(8,128)(2,1)S(1)}, u32[]{:S(2)}, u32[]{:S(2)}) collective-permute-start(bf16[768,128]{1,0:T(8,128)(2,1)S(1)} %pad_maximum_fusion.4), channel_id=1, source_target_pairs={{0,32},{32,64},{64,96},{96,128},{128,160},{160,192},{192,224},{224... | collective-permute-start | bytes 589832 | tf_op jit(solution)/shard_map/ppermute | solution.py:109
  98.3 1.4 collective-permute-done.1
  99.8 3.8 %collective-permute-start.2 = (bf16[768,128]{1,0:T(8,128)(2,1)S(1)}, bf16[768,128]{1,0:T(8,128)(2,1)S(1)}, u32[]{:S(2)}, u32[]{:S(2)}) collective-permute-start(bf16[768,128]{1,0:T(8,128)(2,1)S(1)} %fusion.25), channel_id=1, source_target_pairs={{0,32},{32,64},{64,96},{96,128},{128,160},{160,192},{192,224},{224... | collective-permute-start | bytes 589832 | tf_op jit(solution)/shard_map/ppermute | solution.py:109
  104.0 3.8 %collective-permute-start.10 = (bf16[768,128]{1,0:T(8,128)(2,1)S(1)}, bf16[768,128]{1,0:T(8,128)(2,1)S(1)}, u32[]{:S(2)}, u32[]{:S(2)}) collective-permute-start(bf16[768,128]{1,0:T(8,128)(2,1)S(1)} %fusion.20), channel_id=1, source_target_pairs={{0,32},{32,64},{64,96},{96,128},{128,160},{160,192},{192,224},{224... | collective-permute-start | bytes 589832 | tf_op jit(solution)/shard_map/ppermute | solution.py:109
  108.3 3.8 %collective-permute-start.3 = (bf16[768,128]{1,0:T(8,128)(2,1)S(1)}, bf16[768,128]{1,0:T(8,128)(2,1)S(1)}, u32[]{:S(2)}, u32[]{:S(2)}) collective-permute-start(bf16[768,128]{1,0:T(8,128)(2,1)S(1)} %fusion.26), channel_id=1, source_target_pairs={{0,32},{32,64},{64,96},{96,128},{128,160},{160,192},{192,224},{224... | collective-permute-start | bytes 589832 | tf_op jit(solution)/shard_map/ppermute | solution.py:109
  112.2 0.9 collective-permute-done.10
  113.2 3.8 %collective-permute-start.11 = (bf16[768,128]{1,0:T(8,128)(2,1)S(1)}, bf16[768,128]{1,0:T(8,128)(2,1)S(1)}, u32[]{:S(2)}, u32[]{:S(2)}) collective-permute-start(bf16[768,128]{1,0:T(8,128)(2,1)S(1)} %fusion.21), channel_id=1, source_target_pairs={{0,32},{32,64},{64,96},{96,128},{128,160},{160,192},{192,224},{224... | collective-permute-start | bytes 589832 | tf_op jit(solution)/shard_map/ppermute | solution.py:109
  117.0 0.3 collective-permute-start.15
  117.3 2.4 %collective-permute-done.7 = bf16[768,128]{1,0:T(8,128)(2,1)S(1)} collective-permute-done((bf16[768,128]{1,0:T(8,128)(2,1)S(1)}, bf16[768,128]{1,0:T(8,128)(2,1)S(1)}, u32[]{:S(2)}, u32[]{:S(2)}) %collective-permute-start.7) | collective-permute-done | bytes 196640 | tf_op jit(solution)/shard_map/ppermute | solution.py:110
  119.8 0.3 collective-permute-done.11
  120.1 4.1 %collective-permute-done.15 = bf16[768,128]{1,0:T(8,128)(2,1)S(1)} collective-permute-done((bf16[768,128]{1,0:T(8,128)(2,1)S(1)}, bf16[768,128]{1,0:T(8,128)(2,1)S(1)}, u32[]{:S(2)}, u32[]{:S(2)}) %collective-permute-start.15) | collective-permute-done | bytes 196640 | tf_op jit(solution)/shard_map/ppermute | solution.py:110
  124.4 0.6 fusion.4
  125.0 5.5 %fusion.60 = (bf16[2304,160]{0,1:T(8,128)(2,1)S(1)}, f32[2304,160]{0,1:T(8,128)S(1)}) fusion(bf16[2304,1536]{1,0:T(8,128)(2,1)} %bitcast.118, bf16[1536,160]{0,1:T(8,128)(2,1)S(1)} %bitcast.119), kind=kOutput, calls=%fused_computation.182 | convolution fusion | flops 1132830720 | bytes 9781248 | tf_op jit(solution)/shard_map/dot_general | solution.py:202
  131.0 1.9 %collective-permute-start.22 = (bf16[288,128]{0,1:T(8,128)(2,1)S(1)}, bf16[288,128]{0,1:T(8,128)(2,1)S(1)}, u32[]{:S(2)}, u32[]{:S(2)}) collective-permute-start(bf16[288,128]{0,1:T(8,128)(2,1)S(1)} %get-tuple-element.31), channel_id=1, source_target_pairs={{0,1},{1,2},{2,3},{4,5},{5,6},{6,7},{8,9},{9,10},{10,11},{12,13},{... | collective-permute-start | bytes 221192 | tf_op jit(solution)/shard_map/ppermute | solution.py:16
  133.0 3.6 %collective-permute-start.23 = (bf16[288,128]{0,1:T(8,128)(2,1)S(1)}, bf16[288,128]{0,1:T(8,128)(2,1)S(1)}, u32[]{:S(2)}, u32[]{:S(2)}) collective-permute-start(bf16[288,128]{0,1:T(8,128)(2,1)S(1)} %get-tuple-element.32), channel_id=1, source_target_pairs={{1,0},{2,1},{3,2},{5,4},{6,5},{7,6},{9,8},{10,9},{11,10},{13,12},{... | collective-permute-start | bytes 221192 | tf_op jit(solution)/shard_map/ppermute | solution.py:16
  137.1 1.8 %collective-permute-done.23 = bf16[288,128]{0,1:T(8,128)(2,1)S(1)} collective-permute-done((bf16[288,128]{0,1:T(8,128)(2,1)S(1)}, bf16[288,128]{0,1:T(8,128)(2,1)S(1)}, u32[]{:S(2)}, u32[]{:S(2)}) %collective-permute-start.23) | collective-permute-done | bytes 73760 | tf_op jit(solution)/shard_map/ppermute | solution.py:16
  139.6 1.9 %collective-permute-start.25 = (bf16[16,48,128]{2,1,0:T(8,128)(2,1)S(1)}, bf16[16,48,128]{2,1,0:T(8,128)(2,1)S(1)}, u32[]{:S(2)}, u32[]{:S(2)}) collective-permute-start(bf16[16,48,128]{2,1,0:T(8,128)(2,1)S(1)} %bitcast.135), channel_id=1, source_target_pairs={{0,32},{32,64},{64,96},{96,128},{128,160},{160,192},{192,224},{1,3... | collective-permute-start | bytes 589832 | tf_op jit(solution)/shard_map/ppermute | solution.py:16
  141.5 3.9 %collective-permute-start.24 = (bf16[16,48,128]{2,1,0:T(8,128)(2,1)S(1)}, bf16[16,48,128]{2,1,0:T(8,128)(2,1)S(1)}, u32[]{:S(2)}, u32[]{:S(2)}) collective-permute-start(bf16[16,48,128]{2,1,0:T(8,128)(2,1)S(1)} %bitcast.134), channel_id=1, source_target_pairs={{32,0},{64,32},{96,64},{128,96},{160,128},{192,160},{224,192},{33,... | collective-permute-start | bytes 589832 | tf_op jit(solution)/shard_map/ppermute | solution.py:16
  145.7 1.5 collective-permute-done.25
  147.2 3.1 %collective-permute-done.24 = bf16[16,48,128]{2,1,0:T(8,128)(2,1)S(1)} collective-permute-done((bf16[16,48,128]{2,1,0:T(8,128)(2,1)S(1)}, bf16[16,48,128]{2,1,0:T(8,128)(2,1)S(1)}, u32[]{:S(2)}, u32[]{:S(2)}) %collective-permute-start.24) | collective-permute-done | bytes 196640 | tf_op jit(solution)/shard_map/ppermute | solution.py:16
  150.4 3.9 %collective-permute-start.26 = (f32[16,16,128]{2,1,0:T(8,128)S(1)}, f32[16,16,128]{2,1,0:T(8,128)S(1)}, u32[]{:S(2)}, u32[]{:S(2)}) collective-permute-start(f32[16,16,128]{2,1,0:T(8,128)S(1)} %get-tuple-element.65), channel_id=1, source_target_pairs={{4,0},{8,4},{12,8},{16,12},{20,16},{24,20},{28,24},{5,1},{9,5},{13... | collective-permute-start | bytes 393224 | tf_op jit(solution)/shard_map/ppermute | solution.py:16
  154.3 3.4 %collective-permute-start.27 = (f32[16,16,128]{2,1,0:T(8,128)S(1)}, f32[16,16,128]{2,1,0:T(8,128)S(1)}, u32[]{:S(2)}, u32[]{:S(2)}) collective-permute-start(f32[16,16,128]{2,1,0:T(8,128)S(1)} %get-tuple-element.66), channel_id=1, source_target_pairs={{0,4},{4,8},{8,12},{12,16},{16,20},{20,24},{24,28},{1,5},{5,9},{9,... | collective-permute-start | bytes 393224 | tf_op jit(solution)/shard_map/ppermute | solution.py:16
  157.7 2.3 %collective-permute-done.26 = f32[16,16,128]{2,1,0:T(8,128)S(1)} collective-permute-done((f32[16,16,128]{2,1,0:T(8,128)S(1)}, f32[16,16,128]{2,1,0:T(8,128)S(1)}, u32[]{:S(2)}, u32[]{:S(2)}) %collective-permute-start.26) | collective-permute-done | bytes 131104 | tf_op jit(solution)/shard_map/ppermute | solution.py:16
  160.1 3.5 %collective-permute-done.27 = f32[16,16,128]{2,1,0:T(8,128)S(1)} collective-permute-done((f32[16,16,128]{2,1,0:T(8,128)S(1)}, f32[16,16,128]{2,1,0:T(8,128)S(1)}, u32[]{:S(2)}, u32[]{:S(2)}) %collective-permute-start.27) | collective-permute-done | bytes 131104 | tf_op jit(solution)/shard_map/ppermute | solution.py:16
  163.6 0.7 fusion.32
  (117 shorter events, 6.6 us)
Async XLA Ops:
  0.9 30.5 %collective-permute-start.17 = (bf16[16,16,128]{2,1,0:T(8,128)(2,1)S(1)}, bf16[16,16,128]{2,1,0:T(8,128)(2,1)S(1)}, u32[]{:S(2)}, u32[]{:S(2)}) collective-permute-start(bf16[16,16,128]{2,1,0:T(8,128)(2,1)S(1)} %convert_element_type.270), channel_id=1, source_target_pairs={{4,0},{8,4},{12,8},{16,12},{20,16},{24,20},{28,24},{5,1},{9,5},{13... | collective-permute-start | bytes 196616 | tf_op jit(solution)/shard_map/ppermute | solution.py:16
  5.1 26.4 %collective-permute-start.16 = (bf16[16,16,128]{2,1,0:T(8,128)(2,1)S(1)}, bf16[16,16,128]{2,1,0:T(8,128)(2,1)S(1)}, u32[]{:S(2)}, u32[]{:S(2)}) collective-permute-start(bf16[16,16,128]{2,1,0:T(8,128)(2,1)S(1)} %convert_element_type.270), channel_id=1, source_target_pairs={{0,4},{4,8},{8,12},{12,16},{16,20},{20,24},{24,28},{1,5},{5,9},{9,... | collective-permute-start | bytes 196616 | tf_op jit(solution)/shard_map/ppermute | solution.py:16
  14.4 7.6 %copy-start.1 = (f32[6,3,31]{2,1,0:T(4,128)S(1)}, f32[6,3,31]{2,1,0:T(4,128)}, u32[]{:S(2)}) copy-start(f32[6,3,31]{2,1,0:T(4,128)} %param.6) | copy-start | bytes 6700
  14.4 44.1 %all-to-all-start = ((bf16[8,3,16,16,128]{4,3,2,1,0:T(8,128)(2,1)}), bf16[8,3,16,16,128]{4,3,2,1,0:T(8,128)(2,1)S(1)}, u32[]{:S(2)}, u32[]{:S(2)}) async-start(bf16[8,3,16,16,128]{4,3,2,1,0:T(8,128)(2,1)} %pack.2), calls=%async_computation | async-start | bytes 3145728 | tf_op jit(solution)/shard_map/all_to_all | solution.py:132
  31.5 8.8 %collective-permute-start.19 = (bf16[16,48,128]{2,1,0:T(8,128)(2,1)S(1)}, bf16[16,48,128]{2,1,0:T(8,128)(2,1)S(1)}, u32[]{:S(2)}, u32[]{:S(2)}) collective-permute-start(bf16[16,48,128]{2,1,0:T(8,128)(2,1)S(1)} %pad_maximum_fusion.6), channel_id=1, source_target_pairs={{32,0},{64,32},{96,64},{128,96},{160,128},{192,160},{224,192},{33,... | collective-permute-start | bytes 589832 | tf_op jit(solution)/shard_map/ppermute | solution.py:16
  33.5 8.2 %collective-permute-start.18 = (bf16[16,48,128]{2,1,0:T(8,128)(2,1)S(1)}, bf16[16,48,128]{2,1,0:T(8,128)(2,1)S(1)}, u32[]{:S(2)}, u32[]{:S(2)}) collective-permute-start(bf16[16,48,128]{2,1,0:T(8,128)(2,1)S(1)} %pad_maximum_fusion.6), channel_id=1, source_target_pairs={{0,32},{32,64},{64,96},{96,128},{128,160},{160,192},{192,224},{1,3... | collective-permute-start | bytes 589832 | tf_op jit(solution)/shard_map/ppermute | solution.py:16
  44.4 7.9 %collective-permute-start.20 = (bf16[288,128]{1,0:T(8,128)(2,1)S(1)}, bf16[288,128]{1,0:T(8,128)(2,1)S(1)}, u32[]{:S(2)}, u32[]{:S(2)}) collective-permute-start(bf16[288,128]{1,0:T(8,128)(2,1)S(1)} %concatenate.63), channel_id=1, source_target_pairs={{0,1},{1,2},{2,3},{4,5},{5,6},{6,7},{8,9},{9,10},{10,11},{12,13},{... | collective-permute-start | bytes 221192 | tf_op jit(solution)/shard_map/ppermute | solution.py:16
  48.7 5.6 %collective-permute-start.21 = (bf16[288,128]{1,0:T(8,128)(2,1)S(1)}, bf16[288,128]{1,0:T(8,128)(2,1)S(1)}, u32[]{:S(2)}, u32[]{:S(2)}) collective-permute-start(bf16[288,128]{1,0:T(8,128)(2,1)S(1)} %concatenate.65), channel_id=1, source_target_pairs={{1,0},{2,1},{3,2},{5,4},{6,5},{7,6},{9,8},{10,9},{11,10},{13,12},{... | collective-permute-start | bytes 221192 | tf_op jit(solution)/shard_map/ppermute | solution.py:16
  53.2 4.7 %copy-start.2 = (bf16[2304,16]{1,0:T(8,128)(2,1)}, bf16[2304,16]{1,0:T(8,128)(2,1)S(1)}, u32[]{:S(2)}) copy-start(bf16[2304,16]{1,0:T(8,128)(2,1)S(1)} %slice_dynamic-update-slice_fusion.8) | copy-start | bytes 221188
  58.6 25.6 %all-to-all-start.1 = ((bf16[8,3,16,16,128]{4,3,2,1,0:T(8,128)(2,1)}), bf16[8,3,16,16,128]{4,3,2,1,0:T(8,128)(2,1)S(1)}, u32[]{:S(2)}, u32[]{:S(2)}) async-start(bf16[8,3,16,16,128]{4,3,2,1,0:T(8,128)(2,1)} %pack.3), calls=%async_computation.1 | async-start | bytes 3145728 | tf_op jit(solution)/shard_map/all_to_all | solution.py:132
  75.7 15.5 %collective-permute-start = (bf16[384,128]{1,0:T(8,128)(2,1)S(1)}, bf16[384,128]{1,0:T(8,128)(2,1)S(1)}, u32[]{:S(2)}, u32[]{:S(2)}) collective-permute-start(bf16[384,128]{1,0:T(8,128)(2,1)S(1)} %get-tuple-element.18), channel_id=1, source_target_pairs={{0,32},{32,64},{64,96},{96,128},{128,160},{160,192},{192,224},{224... | collective-permute-start | bytes 294920 | tf_op jit(solution)/shard_map/ppermute | solution.py:97
  79.4 15.1 %collective-permute-start.4 = (bf16[384,128]{1,0:T(8,128)(2,1)S(1)}, bf16[384,128]{1,0:T(8,128)(2,1)S(1)}, u32[]{:S(2)}, u32[]{:S(2)}) collective-permute-start(bf16[384,128]{1,0:T(8,128)(2,1)S(1)} %get-tuple-element.19), channel_id=1, source_target_pairs={{32,0},{64,32},{96,64},{128,96},{160,128},{192,160},{224,192},{0,2... | collective-permute-start | bytes 294920 | tf_op jit(solution)/shard_map/ppermute | solution.py:98
  87.3 7.5 %collective-permute-start.8 = (bf16[384,128]{1,0:T(8,128)(2,1)S(1)}, bf16[384,128]{1,0:T(8,128)(2,1)S(1)}, u32[]{:S(2)}, u32[]{:S(2)}) collective-permute-start(bf16[384,128]{1,0:T(8,128)(2,1)S(1)} %get-tuple-element.27), channel_id=1, source_target_pairs={{0,32},{32,64},{64,96},{96,128},{128,160},{160,192},{192,224},{224... | collective-permute-start | bytes 294920 | tf_op jit(solution)/shard_map/ppermute | solution.py:97
  91.2 7.0 %collective-permute-start.12 = (bf16[384,128]{1,0:T(8,128)(2,1)S(1)}, bf16[384,128]{1,0:T(8,128)(2,1)S(1)}, u32[]{:S(2)}, u32[]{:S(2)}) collective-permute-start(bf16[384,128]{1,0:T(8,128)(2,1)S(1)} %get-tuple-element.28), channel_id=1, source_target_pairs={{32,0},{64,32},{96,64},{128,96},{160,128},{192,160},{224,192},{0,2... | collective-permute-start | bytes 294920 | tf_op jit(solution)/shard_map/ppermute | solution.py:98
  91.3 8.4 %collective-permute-start.1 = (bf16[768,128]{1,0:T(8,128)(2,1)S(1)}, bf16[768,128]{1,0:T(8,128)(2,1)S(1)}, u32[]{:S(2)}, u32[]{:S(2)}) collective-permute-start(bf16[768,128]{1,0:T(8,128)(2,1)S(1)} %pad_maximum_fusion.2), channel_id=1, source_target_pairs={{0,32},{32,64},{64,96},{96,128},{128,160},{160,192},{192,224},{224... | collective-permute-start | bytes 589832 | tf_op jit(solution)/shard_map/ppermute | solution.py:109
  94.6 8.9 %collective-permute-start.5 = (bf16[768,128]{1,0:T(8,128)(2,1)S(1)}, bf16[768,128]{1,0:T(8,128)(2,1)S(1)}, u32[]{:S(2)}, u32[]{:S(2)}) collective-permute-start(bf16[768,128]{1,0:T(8,128)(2,1)S(1)} %pad_maximum_fusion.3), channel_id=1, source_target_pairs={{32,0},{64,32},{96,64},{128,96},{160,128},{192,160},{224,192},{0,2... | collective-permute-start | bytes 589832 | tf_op jit(solution)/shard_map/ppermute | solution.py:110
  94.8 9.1 %collective-permute-start.9 = (bf16[768,128]{1,0:T(8,128)(2,1)S(1)}, bf16[768,128]{1,0:T(8,128)(2,1)S(1)}, u32[]{:S(2)}, u32[]{:S(2)}) collective-permute-start(bf16[768,128]{1,0:T(8,128)(2,1)S(1)} %pad_maximum_fusion.4), channel_id=1, source_target_pairs={{0,32},{32,64},{64,96},{96,128},{128,160},{160,192},{192,224},{224... | collective-permute-start | bytes 589832 | tf_op jit(solution)/shard_map/ppermute | solution.py:109
  98.2 9.5 %collective-permute-start.13 = (bf16[768,128]{1,0:T(8,128)(2,1)S(1)}, bf16[768,128]{1,0:T(8,128)(2,1)S(1)}, u32[]{:S(2)}, u32[]{:S(2)}) collective-permute-start(bf16[768,128]{1,0:T(8,128)(2,1)S(1)} %pad_maximum_fusion.5), channel_id=1, source_target_pairs={{32,0},{64,32},{96,64},{128,96},{160,128},{192,160},{224,192},{0,2... | collective-permute-start | bytes 589832 | tf_op jit(solution)/shard_map/ppermute | solution.py:110
  99.8 8.4 %collective-permute-start.2 = (bf16[768,128]{1,0:T(8,128)(2,1)S(1)}, bf16[768,128]{1,0:T(8,128)(2,1)S(1)}, u32[]{:S(2)}, u32[]{:S(2)}) collective-permute-start(bf16[768,128]{1,0:T(8,128)(2,1)S(1)} %fusion.25), channel_id=1, source_target_pairs={{0,32},{32,64},{64,96},{96,128},{128,160},{160,192},{192,224},{224... | collective-permute-start | bytes 589832 | tf_op jit(solution)/shard_map/ppermute | solution.py:109
  103.6 8.4 %collective-permute-start.6 = (bf16[768,128]{1,0:T(8,128)(2,1)S(1)}, bf16[768,128]{1,0:T(8,128)(2,1)S(1)}, u32[]{:S(2)}, u32[]{:S(2)}) collective-permute-start(bf16[768,128]{1,0:T(8,128)(2,1)S(1)} %fusion.23), channel_id=1, source_target_pairs={{32,0},{64,32},{96,64},{128,96},{160,128},{192,160},{224,192},{0,2... | collective-permute-start | bytes 589832 | tf_op jit(solution)/shard_map/ppermute | solution.py:110
  104.0 9.1 %collective-permute-start.10 = (bf16[768,128]{1,0:T(8,128)(2,1)S(1)}, bf16[768,128]{1,0:T(8,128)(2,1)S(1)}, u32[]{:S(2)}, u32[]{:S(2)}) collective-permute-start(bf16[768,128]{1,0:T(8,128)(2,1)S(1)} %fusion.20), channel_id=1, source_target_pairs={{0,32},{32,64},{64,96},{96,128},{128,160},{160,192},{192,224},{224... | collective-permute-start | bytes 589832 | tf_op jit(solution)/shard_map/ppermute | solution.py:109
  107.8 9.1 %collective-permute-start.14 = (bf16[768,128]{1,0:T(8,128)(2,1)S(1)}, bf16[768,128]{1,0:T(8,128)(2,1)S(1)}, u32[]{:S(2)}, u32[]{:S(2)}) collective-permute-start(bf16[768,128]{1,0:T(8,128)(2,1)S(1)} %fusion.18), channel_id=1, source_target_pairs={{32,0},{64,32},{96,64},{128,96},{160,128},{192,160},{224,192},{0,2... | collective-permute-start | bytes 589832 | tf_op jit(solution)/shard_map/ppermute | solution.py:110
  108.3 9.1 %collective-permute-start.3 = (bf16[768,128]{1,0:T(8,128)(2,1)S(1)}, bf16[768,128]{1,0:T(8,128)(2,1)S(1)}, u32[]{:S(2)}, u32[]{:S(2)}) collective-permute-start(bf16[768,128]{1,0:T(8,128)(2,1)S(1)} %fusion.26), channel_id=1, source_target_pairs={{0,32},{32,64},{64,96},{96,128},{128,160},{160,192},{192,224},{224... | collective-permute-start | bytes 589832 | tf_op jit(solution)/shard_map/ppermute | solution.py:109
  112.1 7.6 %collective-permute-start.7 = (bf16[768,128]{1,0:T(8,128)(2,1)S(1)}, bf16[768,128]{1,0:T(8,128)(2,1)S(1)}, u32[]{:S(2)}, u32[]{:S(2)}) collective-permute-start(bf16[768,128]{1,0:T(8,128)(2,1)S(1)} %fusion.24), channel_id=1, source_target_pairs={{32,0},{64,32},{96,64},{128,96},{160,128},{192,160},{224,192},{0,2... | collective-permute-start | bytes 589832 | tf_op jit(solution)/shard_map/ppermute | solution.py:110
  113.2 7.0 %collective-permute-start.11 = (bf16[768,128]{1,0:T(8,128)(2,1)S(1)}, bf16[768,128]{1,0:T(8,128)(2,1)S(1)}, u32[]{:S(2)}, u32[]{:S(2)}) collective-permute-start(bf16[768,128]{1,0:T(8,128)(2,1)S(1)} %fusion.21), channel_id=1, source_target_pairs={{0,32},{32,64},{64,96},{96,128},{128,160},{160,192},{192,224},{224... | collective-permute-start | bytes 589832 | tf_op jit(solution)/shard_map/ppermute | solution.py:109
  117.0 7.2 %collective-permute-start.15 = (bf16[768,128]{1,0:T(8,128)(2,1)S(1)}, bf16[768,128]{1,0:T(8,128)(2,1)S(1)}, u32[]{:S(2)}, u32[]{:S(2)}) collective-permute-start(bf16[768,128]{1,0:T(8,128)(2,1)S(1)} %fusion.19), channel_id=1, source_target_pairs={{32,0},{64,32},{96,64},{128,96},{160,128},{192,160},{224,192},{0,2... | collective-permute-start | bytes 589832 | tf_op jit(solution)/shard_map/ppermute | solution.py:110
  119.7 4.6 %copy-start.3 = (bf16[1536,160]{0,1:T(8,128)(2,1)S(1)}, bf16[1536,160]{0,1:T(8,128)(2,1)}, u32[]{:S(2)}) copy-start(bf16[1536,160]{0,1:T(8,128)(2,1)} %convolution_convert_fusion) | copy-start | bytes 1474564
  119.7 4.6 %copy-start.4 = (bf16[6,160,128]{2,0,1:T(8,128)(2,1)S(1)}, bf16[6,160,128]{2,0,1:T(8,128)(2,1)}, u32[]{:S(2)}) copy-start(bf16[6,160,128]{2,0,1:T(8,128)(2,1)} %fusion) | copy-start | bytes 737284
  131.0 5.9 %collective-permute-start.22 = (bf16[288,128]{0,1:T(8,128)(2,1)S(1)}, bf16[288,128]{0,1:T(8,128)(2,1)S(1)}, u32[]{:S(2)}, u32[]{:S(2)}) collective-permute-start(bf16[288,128]{0,1:T(8,128)(2,1)S(1)} %get-tuple-element.31), channel_id=1, source_target_pairs={{0,1},{1,2},{2,3},{4,5},{5,6},{6,7},{8,9},{9,10},{10,11},{12,13},{... | collective-permute-start | bytes 221192 | tf_op jit(solution)/shard_map/ppermute | solution.py:16
  133.0 5.8 %collective-permute-start.23 = (bf16[288,128]{0,1:T(8,128)(2,1)S(1)}, bf16[288,128]{0,1:T(8,128)(2,1)S(1)}, u32[]{:S(2)}, u32[]{:S(2)}) collective-permute-start(bf16[288,128]{0,1:T(8,128)(2,1)S(1)} %get-tuple-element.32), channel_id=1, source_target_pairs={{1,0},{2,1},{3,2},{5,4},{6,5},{7,6},{9,8},{10,9},{11,10},{13,12},{... | collective-permute-start | bytes 221192 | tf_op jit(solution)/shard_map/ppermute | solution.py:16
  139.6 7.6 %collective-permute-start.25 = (bf16[16,48,128]{2,1,0:T(8,128)(2,1)S(1)}, bf16[16,48,128]{2,1,0:T(8,128)(2,1)S(1)}, u32[]{:S(2)}, u32[]{:S(2)}) collective-permute-start(bf16[16,48,128]{2,1,0:T(8,128)(2,1)S(1)} %bitcast.135), channel_id=1, source_target_pairs={{0,32},{32,64},{64,96},{96,128},{128,160},{160,192},{192,224},{1,3... | collective-permute-start | bytes 589832 | tf_op jit(solution)/shard_map/ppermute | solution.py:16
  141.5 8.8 %collective-permute-start.24 = (bf16[16,48,128]{2,1,0:T(8,128)(2,1)S(1)}, bf16[16,48,128]{2,1,0:T(8,128)(2,1)S(1)}, u32[]{:S(2)}, u32[]{:S(2)}) collective-permute-start(bf16[16,48,128]{2,1,0:T(8,128)(2,1)S(1)} %bitcast.134), channel_id=1, source_target_pairs={{32,0},{64,32},{96,64},{128,96},{160,128},{192,160},{224,192},{33,... | collective-permute-start | bytes 589832 | tf_op jit(solution)/shard_map/ppermute | solution.py:16
  145.4 18.1 %copy-start = (f32[16,16,128]{2,1,0:T(8,128)S(1)}, f32[16,16,128]{2,1,0:T(8,128)}, u32[]{:S(2)}) copy-start(f32[16,16,128]{2,1,0:T(8,128)} %param.7) | copy-start | bytes 393220
  150.4 9.7 %collective-permute-start.26 = (f32[16,16,128]{2,1,0:T(8,128)S(1)}, f32[16,16,128]{2,1,0:T(8,128)S(1)}, u32[]{:S(2)}, u32[]{:S(2)}) collective-permute-start(f32[16,16,128]{2,1,0:T(8,128)S(1)} %get-tuple-element.65), channel_id=1, source_target_pairs={{4,0},{8,4},{12,8},{16,12},{20,16},{24,20},{28,24},{5,1},{9,5},{13... | collective-permute-start | bytes 393224 | tf_op jit(solution)/shard_map/ppermute | solution.py:16
  154.3 9.3 %collective-permute-start.27 = (f32[16,16,128]{2,1,0:T(8,128)S(1)}, f32[16,16,128]{2,1,0:T(8,128)S(1)}, u32[]{:S(2)}, u32[]{:S(2)}) collective-permute-start(f32[16,16,128]{2,1,0:T(8,128)S(1)} %get-tuple-element.66), channel_id=1, source_target_pairs={{0,4},{4,8},{8,12},{12,16},{16,20},{20,24},{24,28},{1,5},{5,9},{9,... | collective-permute-start | bytes 393224 | tf_op jit(solution)/shard_map/ppermute | solution.py:16

commit v3 on v0

--- a/solution.py
+++ b/solution.py
@@ -1,10 +1,16 @@
+import functools
+
 import jax
 import jax.numpy as jnp
 from jax import lax
+from jax.experimental import pallas as pl
+from jax.experimental.pallas import tpu as pltpu
 from jax.sharding import PartitionSpec as P
 
 background_level = 0.1
 highest = lax.Precision.HIGHEST
+capacity = 2
+usual_slots = 56
 
 
 def shift(value, axis, step):
@@ -29,42 +35,164 @@
     return jnp.concatenate([value[:, g * width : (g + 1) * width] for g in range(groups)], axis=0)
 
 
-def route_tiles(recorded, tile_place, positions):
-    view_count, slot_count = recorded.shape[:2]
-    tile_width = recorded.shape[2] * recorded.shape[3] * recorded.shape[4]
+def slot_tables(tile_place, positions, chunks, usual):
+    view_count = tile_place.shape[0]
+    gz_count, gy_count = lax.axis_size("gz"), lax.axis_size("gy")
+    my_gz, my_gy = lax.axis_index("gz"), lax.axis_index("gy")
+    chunk = view_count // chunks
+    placed = tile_place.reshape(view_count, gz_count, gy_count, -1)
+    slot_count = placed.shape[-1]
+    entries = view_count * slot_count
+    group = lax.dynamic_index_in_dim(placed, my_gz, 1, keepdims=False)
+    group = group.transpose(1, 0, 2).reshape(gy_count, entries)
+    destination = group // positions
+    dest_gy = destination % gy_count
+    ahead = (destination // gy_count - my_gz) % gz_count
+    view = jnp.arange(entries) // slot_count % chunk
+    cell = (ahead * chunk + view) * positions + group % positions
+    own_dest = lax.dynamic_index_in_dim(dest_gy, my_gy, 0, keepdims=True)
+    sends = own_dest == jnp.arange(gy_count)[:, None]
+    takes = dest_gy == my_gy
+    number = jnp.broadcast_to(jnp.arange(entries)[None, :], takes.shape)
+    chosen = jnp.stack([sends, takes])
+    value = jnp.stack([number, cell])
+    upto = (jnp.arange(entries)[:, None] <= jnp.arange(entries)[None, :]).astype(jnp.bfloat16)
+    rank = jnp.dot(chosen.astype(jnp.bfloat16), upto, preferred_element_type=jnp.float32)
+    rank = jnp.where(chosen, rank.astype(jnp.int32) - 1, -1)
+
+    def table(first, lanes):
+        hit = rank[..., None, :] == first + jnp.arange(lanes)[:, None]
+        return jnp.sum(jnp.where(hit, value[..., None, :], 0), axis=-1).astype(jnp.int32)
+
+    ends = [
+        jnp.sum(takes[:, : c * chunk * slot_count], axis=-1).astype(jnp.int32)
+        for c in range(chunks + 1)
+    ]
+    return table, jnp.stack(ends)
+
+
+def most_slots(tile_place, positions):
+    gy_count = lax.axis_size("gy")
     route_count = lax.axis_size(("gz", "gy"))
-    my_index = lax.axis_index(("gz", "gy"))
-    capacity = max(2, 2 * slot_count // route_count)
-    placed = tile_place.reshape(view_count, route_count, slot_count)
-    destination = placed // positions
-    position = placed % positions
-    matching = destination[..., :, None] == destination[..., None, :]
-    earlier = jnp.arange(slot_count)[None, :] < jnp.arange(slot_count)[:, None]
-    ranking = jnp.sum(matching & earlier, axis=-1)
-    my_dest = lax.dynamic_index_in_dim(destination, my_index, 1, keepdims=False)
-    my_rank = lax.dynamic_index_in_dim(ranking, my_index, 1, keepdims=False)
-    target = my_dest * capacity + my_rank
-    picker = (jnp.arange(route_count * capacity)[None, :, None] == target[:, None, :]).astype(
-        jnp.bfloat16
-    )
-    outgoing = jnp.einsum(
-        "vbs,vsk->vbk",
-        picker,
-        recorded.reshape(view_count, slot_count, tile_width),
-        preferred_element_type=jnp.float32,
-    ).astype(jnp.bfloat16)
-    arrived = lax.all_to_all(outgoing, ("gz", "gy"), split_axis=1, concat_axis=1, tiled=True)
-    owned_here = destination == my_index
-    at_position = ((position[..., None] == jnp.arange(positions)) & owned_here[..., None]).astype(
-        jnp.float32
-    )
-    at_rank = (ranking[..., None] == jnp.arange(capacity)).astype(jnp.float32)
-    placer = (
-        jnp.einsum("vrsp,vrsc->vprc", at_position, at_rank)
-        .reshape(view_count, positions, route_count * capacity)
-        .astype(jnp.bfloat16)
-    )
-    return jnp.einsum("vpb,vbk->vpk", placer, arrived, preferred_element_type=jnp.float32)
+    dest_gy = (tile_place // positions) % gy_count
+    dest_gy = dest_gy.reshape(tile_place.shape[0], route_count, 1, -1)
+    return jnp.max(jnp.sum(dest_gy == jnp.arange(gy_count)[:, None], axis=(0, 3)))
+
+
+def pack_kernel(source, tiles, outgoing):
+    partners, lanes = outgoing.shape[:2]
+    for partner in range(partners):
+        for lane in range(lanes):
+            outgoing[partner, lane] = tiles[source[partner, lane]]
+
+
+def join_kernel(chunk, ends, cell, late_cell, arrived, late, *blocks_and_total):
+    blocks, total = blocks_and_total[:-1], blocks_and_total[-1]
+    partners, usual = arrived.shape[:2]
+    step = 16
+
+    def clear(index, carry):
+        total[pl.ds(index * step, step)] = jnp.zeros((step,) + total.shape[1:], total.dtype)
+        return carry
+
+    lax.fori_loop(0, total.shape[0] // step, clear, 0)
+
+    def add(cells, tiles, partner, lane):
+        place = cells[partner, lane]
+        total[place] = add_rounded(total[place], tiles[partner, lane])
+
+    for partner in range(partners):
+        first, last = ends[chunk, partner], ends[chunk + 1, partner]
+
+        def add_usual(lane, carry):
+            add(cell, arrived, partner, lane)
+            return carry
+
+        def add_late(lane, carry):
+            add(late_cell, late, partner, lane - usual)
+            return carry
+
+        lax.fori_loop(jnp.minimum(first, usual), jnp.minimum(last, usual), add_usual, 0)
+        lax.fori_loop(jnp.maximum(first, usual), jnp.maximum(last, usual), add_late, 0)
+    start = 0
+    for block in blocks:
+        block[...] = total[start : start + block.shape[0]]
+        start += block.shape[0]
+
+
+smem = pl.BlockSpec(memory_space=pltpu.SMEM)
+vmem = pl.BlockSpec(memory_space=pltpu.VMEM)
+
+
+def pack(source, tiles):
+    return pl.pallas_call(
+        pack_kernel,
+        out_shape=jax.ShapeDtypeStruct(source.shape + tiles.shape[1:], tiles.dtype),
+        in_specs=[smem, vmem],
+        out_specs=vmem,
+        compiler_params=pltpu.CompilerParams(vmem_limit_bytes=32 << 20),
+        name="pack",
+    )(source, tiles)
+
+
+def join(chunk, ends, cell, late_cell, arrived, late, devices, cells):
+    tile = arrived.shape[2:]
+    half = devices // 2
+    sizes = [cells] * half + [cells // 2] * 2 + [cells] * (half - 1)
+    return pl.pallas_call(
+        functools.partial(join_kernel, chunk),
+        out_shape=[jax.ShapeDtypeStruct((size,) + tile, arrived.dtype) for size in sizes],
+        in_specs=[smem, smem, smem, vmem, vmem],
+        out_specs=[vmem] * len(sizes),
+        scratch_shapes=[pltpu.VMEM((devices * cells,) + tile, arrived.dtype)],
+        compiler_params=pltpu.CompilerParams(vmem_limit_bytes=32 << 20),
+        name="join",
+    )(ends, cell, late_cell, arrived, late)
+
+
+def exchange(value):
+    return lax.all_to_all(value, "gy", split_axis=0, concat_axis=0, tiled=True)
+
+
+def exchange_by_permutes(value):
+    devices, me = lax.axis_size("gy"), lax.axis_index("gy")
+    result = value
+    for step in range(1, devices):
+        part = lax.dynamic_index_in_dim(value, (me + step) % devices, 0)
+        part = lax.ppermute(part, "gy", [(i, (i + step) % devices) for i in range(devices)])
+        result = lax.dynamic_update_index_in_dim(result, part, (me - step) % devices, 0)
+    return result
+
+
+def add_rounded(left, right):
+    return (left.astype(jnp.float32) + right.astype(jnp.float32)).astype(left.dtype)
+
+
+def ring_sum(blocks):
+    devices = len(blocks) - 1
+    half = devices // 2
+    up = [(i, (i + 1) % devices) for i in range(devices)]
+    down = [(j, i) for i, j in up]
+    middle = blocks[half].shape[0]
+    from_below = lax.ppermute(blocks[half], "gz", up)
+    from_above = lax.ppermute(blocks[half + 1], "gz", down)
+    for ahead in range(half - 1, 0, -1):
+        upward, downward = blocks[ahead], blocks[devices - ahead + 1]
+        if ahead == half - 1:
+            upward = jnp.concatenate([add_rounded(upward[:middle], from_below), upward[middle:]])
+            downward = jnp.concatenate(
+                [downward[:middle], add_rounded(downward[middle:], from_above)]
+            )
+        else:
+            upward = add_rounded(upward, from_below)
+            downward = add_rounded(downward, from_above)
+        from_below = lax.ppermute(upward, "gz", up)
+        from_above = lax.ppermute(downward, "gz", down)
+    return (
+        blocks[0].astype(jnp.float32)
+        + from_below.astype(jnp.float32)
+        + from_above.astype(jnp.float32)
+    )
 
 
 def on_device(recorded, tile_place, psf, estimate):
@@ -77,7 +205,17 @@
     radius = (psf.shape[2] - 1) // 2
     side = 16
     tall, wide = depth + 2 * side, rows + 2 * side
-    joined = route_tiles(recorded, tile_place, positions).reshape(view_count, area, cols)
+    chunks = 2
+    chunk = view_count // chunks
+    gz_count, gy_count = lax.axis_size("gz"), lax.axis_size("gy")
+    tiles = recorded.reshape(-1, tile_depth * tile_rows, cols)
+    lanes = gz_count * capacity * view_count
+    usual = min(usual_slots, lanes)
+    table, ends = slot_tables(tile_place, positions, chunks, usual)
+    usual_table = table(0, usual)
+    outgoing, psf = lax.optimization_barrier((pack(usual_table[0], tiles), psf))
+    arrived = exchange(outgoing)
+    own = estimate.astype(jnp.bfloat16)
 
     kernels = psf / jnp.sum(psf, axis=-1, keepdims=True)
     line = jnp.arange(area)
@@ -98,7 +236,19 @@
         kernels[:, 2], column[:, None] - jnp.arange(cols)[None, :] + radius
     ).astype(jnp.bfloat16)
 
-    own = estimate.astype(jnp.bfloat16)
+    own, tile_place, _ = lax.optimization_barrier((own, tile_place, sheet))
+
+    def late_exchange():
+        late_table = table(usual, lanes - usual)
+        return exchange_by_permutes(pack(late_table[0], tiles)), late_table[1]
+
+    def no_exchange():
+        shape = (gy_count, lanes - usual)
+        return jnp.zeros(shape + tiles.shape[1:], tiles.dtype), jnp.zeros(shape, jnp.int32)
+
+    late, late_cell = lax.cond(
+        most_slots(tile_place, positions) > usual, late_exchange, no_exchange
+    )
     own = jnp.concatenate([shift(own, "gy", 1), own, shift(own, "gy", -1)], axis=1)
     own = jnp.concatenate([shift(own, "gz", 1), own, shift(own, "gz", -1)], axis=0)
     own = own.reshape(tall * wide, cols)
@@ -111,6 +261,12 @@
     )
     swept = swept.astype(jnp.bfloat16).reshape(view_count, area, -1)
     blurred = jnp.einsum("vac,vck->vak", swept, col_taps, preferred_element_type=jnp.float32)
+    joined = [
+        ring_sum(join(c, ends, usual_table[1], late_cell, arrived, late, gz_count, chunk * positions))
+        for c in range(chunks)
+    ]
+    joined = jnp.concatenate(joined).reshape(view_count, area, cols)
+
     ratio = (joined / (blurred + background_level)).astype(jnp.bfloat16)
 
     spread = jnp.einsum("vak,vck->vac", ratio, col_taps, preferred_element_type=jnp.float32)
@@ -126,9 +282,9 @@
     upper = shift(total[:side].astype(jnp.bfloat16), "gz", -1)
     lower = shift(total[tall - side :].astype(jnp.bfloat16), "gz", 1)
     total = total[side : side + depth] + upper.astype(jnp.float32) + lower.astype(jnp.float32)
-    upper = shift(total[:, :side].astype(jnp.bfloat16), "gy", -1)
-    lower = shift(total[:, wide - side :].astype(jnp.bfloat16), "gy", 1)
-    total = total[:, side : side + rows] + upper.astype(jnp.float32) + lower.astype(jnp.float32)
+    upper = shift(total[:, :side], "gy", -1)
+    lower = shift(total[:, wide - side :], "gy", 1)
+    total = total[:, side : side + rows] + upper + lower
     return estimate * total / view_count
 
 

time: 191 us -> 144 us (0.75)
  waiting for transfers between devices: 95 us -> 30.8 us
  starting transfers between devices: 52.6 us -> 69.2 us
  matrix products: 20.5 us -> 9.83 us
  Pallas kernels: 0 us -> 8.38 us
    ppermute x12, waiting for transfers between devices: 95 us -> 18.8 us  [shift(): return lax.ppermute(value, axis, pairs)]
    ppermute x0 -> x16, starting transfers between devices: none -> 22.7 us  [the longest x6 17.8 us: ring_sum(): from_below = lax.ppermute(upward, 'gz', up)]
    ppermute x0 -> x16, waiting for transfers between devices: none -> 12.1 us  [the longest x6 6.58 us: ring_sum(): from_above = lax.ppermute(downward, 'gz', down)]
    pallas_call x0 -> x3, Pallas kernels: none -> 8.38 us  [the longest x2 6.74 us: join(): pl.pallas_call(functools.partial(join_kernel, chunk), out_shape=[jax.Shap...]
    all_to_all x1, starting transfers between devices: 13.7 us -> 5.68 us  [exchange(): return lax.all_to_all(value, 'gy', split_axis=0, concat_axis=0, tiled=True)]
    dot_general x3 -> x2, matrix products: 7.85 us -> 0.59 us  [the longest x1 0.43 us: on_device(): jnp.einsum('vac,vck->vak', swept, col_taps, preferred_element_type=jnp.fl...]
    convert_element_type x1 -> x0, local copies, waits for them, and re-layouts: 3.8 us -> none  [route_tiles(): outgoing = jnp.einsum('vbs,vsk->vbk', picker, recorded.reshape(view_count...]
    dot_general x1, matrix products: 5.46 us -> 2.43 us  [on_device(): total = jnp.dot(sheet, spread, preferred_element_type=jnp.float32)]
  transfers between devices with their start and end apart: 13 -> 29, of which waited for: 8 -> 17; matrix products, arithmetic and copies ran while one was open for 14% -> 11% of each run, Pallas kernels for 0% -> 2%
where the time goes in v3:
time: 144 us; the launch traced here: 142 us
  starting transfers between devices  69.2 us (48%)
  waiting for transfers between devices  30.8 us (21%)
  local copies, waits for them, and re-layouts  11.6 us (8%)
  other arithmetic  10.8 us (8%)
  matrix products  9.83 us (7%)
  Pallas kernels  8.38 us (6%)
  between operations  1.52 us (1%)
    ppermute x12, starting transfers between devices, shift(): return lax.ppermute(value, axis, pairs)  40.9 us
    ppermute x12, waiting for transfers between devices, shift(): return lax.ppermute(value, axis, pairs)  18.8 us
    ppermute x6, starting transfers between devices, ring_sum(): from_below = lax.ppermute(upward, 'gz', up)  17.8 us
    pallas_call x2, Pallas kernels, join(): pl.pallas_call(functools.partial(join_kernel, chunk), out_shape=[jax.Shap...  6.74 us
    ppermute x6, waiting for transfers between devices, ring_sum(): from_above = lax.ppermute(downward, 'gz', down)  6.58 us
    all_to_all x1, starting transfers between devices, exchange(): return lax.all_to_all(value, 'gy', split_axis=0, concat_axis=0, tiled=True)  5.68 us
    convert_element_type x1, other arithmetic, on_device(): sheet = (depth_taps[:, None, :] * row_taps[None, :, :]).astype(jnp.bfloat16)  4.97 us
    ppermute x6, waiting for transfers between devices, ring_sum(): from_below = lax.ppermute(upward, 'gz', up)  4.83 us
  transfers between devices with their start and end apart: 29, of which 17 were waited for; matrix products, arithmetic and copies ran while one was open for 11% of the time, Pallas kernels for 2%

profile of v3, /device:TPU:106, one launch (start us, length us, event | category | flops | bytes accessed | tf_op | source)
XLA Modules:
  0.0 142.2 jit_solution(3992945656720983315)
XLA Ops:
  0.0 1.0 reshape.497
  1.6 0.4 select_reduce_fusion.1
  1.9 1.6 %pack.3 = bf16[8,56,16,128]{3,2,1,0:T(8,128)(2,1)S(1)} custom-call(s32[8,56]{1,0:T(8,128)S(1)} %get-tuple-element.126.source, bf16[288,16,128]{2,1,0:T(8,128)(2,1)} %bitcast.67), custom_call_target="tpu_custom_call" | custom-call | tf_op jit(solution)/shard_map/pack/pallas_call | solution.py:128
  3.6 1.3 copy-done
  5.2 0.6 fusion.1
  5.9 0.6 fusion.2
  6.7 5.0 %multiply_convert_fusion = bf16[48,48,1536]{2,1,0:T(8,128)(2,1)} fusion(f32[48,1536]{1,0:T(8,128)S(1)} %bitcast.75, f32[48,1536]{1,0:T(8,128)S(1)} %bitcast.74), kind=kLoop, calls=%fused_computation.18 | loop fusion | flops 7077888 | bytes 7667712 | tf_op jit(solution)/shard_map/convert_element_type | solution.py:230
  12.1 0.6 reduce_max.9
  13.4 1.3 conditional.1
  13.4 1.3 broadcast.650
  14.7 4.2 %collective-permute-start.23 = (bf16[16,16,128]{2,1,0:T(8,128)(2,1)S(1)}, bf16[16,16,128]{2,1,0:T(8,128)(2,1)S(1)}, u32[]{:S(2)}, u32[]{:S(2)}) collective-permute-start(bf16[16,16,128]{2,1,0:T(8,128)(2,1)S(1)} %convert_element_type.203), channel_id=1, source_target_pairs={{0,4},{4,8},{8,12},{12,16},{16,20},{20,24},{24,28},{1,5},{5,9},{9,... | collective-permute-start | bytes 196616 | tf_op jit(solution)/shard_map/ppermute | solution.py:19
  18.9 4.0 %collective-permute-start.24 = (bf16[16,16,128]{2,1,0:T(8,128)(2,1)S(1)}, bf16[16,16,128]{2,1,0:T(8,128)(2,1)S(1)}, u32[]{:S(2)}, u32[]{:S(2)}) collective-permute-start(bf16[16,16,128]{2,1,0:T(8,128)(2,1)S(1)} %convert_element_type.203), channel_id=1, source_target_pairs={{4,0},{8,4},{12,8},{16,12},{20,16},{24,20},{28,24},{5,1},{9,5},{13... | collective-permute-start | bytes 196616 | tf_op jit(solution)/shard_map/ppermute | solution.py:19
  23.0 5.7 %all-to-all-start = ((bf16[8,56,16,128]{3,2,1,0:T(8,128)(2,1)}), bf16[8,56,16,128]{3,2,1,0:T(8,128)(2,1)S(1)}, u32[]{:S(2)}, u32[]{:S(2)}) async-start(bf16[8,56,16,128]{3,2,1,0:T(8,128)(2,1)} %copy-done), calls=%async_computation | async-start | bytes 3670016 | tf_op jit(solution)/shard_map/all_to_all | solution.py:154
  28.7 0.7 convert_reduce_fusion.1
  29.4 0.5 pad.22.clone
  30.1 0.6 convert_reduce_fusion.2
  30.8 5.0 %collective-permute-start.25 = (bf16[16,48,128]{2,1,0:T(8,128)(2,1)S(1)}, bf16[16,48,128]{2,1,0:T(8,128)(2,1)S(1)}, u32[]{:S(2)}, u32[]{:S(2)}) collective-permute-start(bf16[16,48,128]{2,1,0:T(8,128)(2,1)S(1)} %constant_dynamic-update-slice_fusion.7), channel_id=1, source_target_pairs={{0,32},{32,64},{64,96},{96,128},{128,160},{160,192},{192,224},{1,3... | collective-permute-start | bytes 589832 | tf_op jit(solution)/shard_map/ppermute | solution.py:19
  35.8 2.1 %collective-permute-start.26 = (bf16[16,48,128]{2,1,0:T(8,128)(2,1)S(1)}, bf16[16,48,128]{2,1,0:T(8,128)(2,1)S(1)}, u32[]{:S(2)}, u32[]{:S(2)}) collective-permute-start(bf16[16,48,128]{2,1,0:T(8,128)(2,1)S(1)} %constant_dynamic-update-slice_fusion.7), channel_id=1, source_target_pairs={{32,0},{64,32},{96,64},{128,96},{160,128},{192,160},{224,192},{33,... | collective-permute-start | bytes 589832 | tf_op jit(solution)/shard_map/ppermute | solution.py:19
  37.9 0.9 fusion
  39.0 5.6 %collective-permute-done.26 = bf16[16,48,128]{2,1,0:T(8,128)(2,1)S(1)} collective-permute-done((bf16[16,48,128]{2,1,0:T(8,128)(2,1)S(1)}, bf16[16,48,128]{2,1,0:T(8,128)(2,1)S(1)}, u32[]{:S(2)}, u32[]{:S(2)}) %collective-permute-start.26) | collective-permute-done | bytes 196640 | tf_op jit(solution)/shard_map/ppermute | solution.py:19
  44.7 1.0 fusion.59
  45.6 1.9 %concatenate.63 = bf16[288,128]{1,0:T(8,128)(2,1)} concatenate(bf16[288,16]{1,0:T(8,128)(2,1)} %get-tuple-element.106, bf16[288,16]{1,0:T(8,128)(2,1)} %get-tuple-element.105, bf16[288,16]{1,0:T(8,128)(2,1)} %get-tuple-element.104, bf16[288,16]{1,0:T(8,128)(2,1)} %get-tuple-element.103, bf16[288,16]{1,0:T(8,128)(2,1)} %get-tuple-element.102, bf16[288,16]{1,0:T(8,128)(2,1)} %get-tuple-element.101, ...), dimensions={1} | concatenate | bytes 147456 | tf_op jit(solution)/shard_map/concatenate | solution.py:30
  47.6 1.9 %collective-permute-start.27 = (bf16[288,128]{1,0:T(8,128)(2,1)}, bf16[288,128]{1,0:T(8,128)(2,1)S(1)}, u32[]{:S(2)}, u32[]{:S(2)}) collective-permute-start(bf16[288,128]{1,0:T(8,128)(2,1)} %concatenate.63), channel_id=1, source_target_pairs={{0,1},{1,2},{2,3},{4,5},{5,6},{6,7},{8,9},{9,10},{10,11},{12,13},{... | collective-permute-start | bytes 221192 | tf_op jit(solution)/shard_map/ppermute | solution.py:19
  49.5 0.7 pad_add_fusion.1.ends
  50.2 0.9 concatenate.65
  51.1 3.6 %collective-permute-start.28 = (bf16[288,128]{1,0:T(8,128)(2,1)}, bf16[288,128]{1,0:T(8,128)(2,1)S(1)}, u32[]{:S(2)}, u32[]{:S(2)}) collective-permute-start(bf16[288,128]{1,0:T(8,128)(2,1)} %concatenate.65), channel_id=1, source_target_pairs={{1,0},{2,1},{3,2},{5,4},{6,5},{7,6},{9,8},{10,9},{11,10},{13,12},{... | collective-permute-start | bytes 221192 | tf_op jit(solution)/shard_map/ppermute | solution.py:19
  55.5 1.5 %collective-permute-done.28 = bf16[288,128]{1,0:T(8,128)(2,1)S(1)} collective-permute-done((bf16[288,128]{1,0:T(8,128)(2,1)}, bf16[288,128]{1,0:T(8,128)(2,1)S(1)}, u32[]{:S(2)}, u32[]{:S(2)}) %collective-permute-start.28) | collective-permute-done | bytes 73760 | tf_op jit(solution)/shard_map/ppermute | solution.py:19
  57.8 4.4 %convolution_convert_fusion = bf16[1536,160]{0,1:T(8,128)(2,1)S(1)} fusion(bf16[2304,1536]{1,0:T(8,128)(2,1)} %bitcast.61, bf16[2304,16]{1,0:T(8,128)(2,1)S(1)} %constant_dynamic-update-slice_fusion.18, bf16[2304,16]{1,0:T(8,128)(2,1)S(1)} %constant_dynamic-update-slice_fusion.10, bf16[2304,128]{1,0:T(8,128)(2,1)S(1)} %bitcast.66), kind=kOutput, calls=%fused_computation.21 | convolution fusion | flops 1134919680 | bytes 8306688 | tf_op jit(solution)/shard_map/dot_general | solution.py:259
  62.2 3.3 %join.2 = (bf16[48,16,128]{2,1,0:T(8,128)(2,1)S(1)}, bf16[48,16,128]{2,1,0:T(8,128)(2,1)S(1)}, bf16[48,16,128]{2,1,0:T(8,128)(2,1)S(1)}, bf16[48,16,128]{2,1,0:T...) custom-call(s32[3,8]{1,0:T(4,128)S(1)} %pad_add_fusion.1.ends, ...), custom_call_target="tpu_custom_call" | custom-call | tf_op jit(solution)/shard_map/join/pallas_call | solution.py:142
  65.6 0.4 convolution_add_fusion
  66.1 2.1 %collective-permute-start.11 = (bf16[24,16,128]{2,1,0:T(8,128)(2,1)S(1)}, bf16[24,16,128]{2,1,0:T(8,128)(2,1)S(1)}, u32[]{:S(2)}, u32[]{:S(2)}) collective-permute-start(bf16[24,16,128]{2,1,0:T(8,128)(2,1)S(1)} %get-tuple-element.51), channel_id=1, source_target_pairs={{32,0},{64,32},{96,64},{128,96},{160,128},{192,160},{224,192},{0,2... | collective-permute-start | bytes 294920 | tf_op jit(solution)/shard_map/ppermute | solution.py:178
  68.2 3.5 %join.3 = (bf16[48,16,128]{2,1,0:T(8,128)(2,1)S(1)}, bf16[48,16,128]{2,1,0:T(8,128)(2,1)S(1)}, bf16[48,16,128]{2,1,0:T(8,128)(2,1)S(1)}, bf16[48,16,128]{2,1,0:T...) custom-call(s32[3,8]{1,0:T(4,128)S(1)} %pad_add_fusion.1.ends, ...), custom_call_target="tpu_custom_call" | custom-call | tf_op jit(solution)/shard_map/join/pallas_call | solution.py:142
  71.6 1.2 collective-permute-start.15
  72.8 1.0 collective-permute-start.19
  73.9 2.4 %collective-permute-start.8 = (bf16[48,16,128]{2,1,0:T(8,128)(2,1)S(1)}, bf16[48,16,128]{2,1,0:T(8,128)(2,1)S(1)}, u32[]{:S(2)}, u32[]{:S(2)}) collective-permute-start(bf16[48,16,128]{2,1,0:T(8,128)(2,1)S(1)} %pad_maximum_fusion.2), channel_id=1, source_target_pairs={{0,32},{32,64},{64,96},{96,128},{128,160},{160,192},{192,224},{224... | collective-permute-start | bytes 589832 | tf_op jit(solution)/shard_map/ppermute | solution.py:189
  76.4 0.6 collective-permute-done.15
  77.1 2.7 %collective-permute-start.16 = (bf16[48,16,128]{2,1,0:T(8,128)(2,1)S(1)}, bf16[48,16,128]{2,1,0:T(8,128)(2,1)S(1)}, u32[]{:S(2)}, u32[]{:S(2)}) collective-permute-start(bf16[48,16,128]{2,1,0:T(8,128)(2,1)S(1)} %pad_maximum_fusion.4), channel_id=1, source_target_pairs={{0,32},{32,64},{64,96},{96,128},{128,160},{160,192},{192,224},{224... | collective-permute-start | bytes 589832 | tf_op jit(solution)/shard_map/ppermute | solution.py:189
  80.0 1.7 %collective-permute-done.8 = bf16[48,16,128]{2,1,0:T(8,128)(2,1)S(1)} collective-permute-done((bf16[48,16,128]{2,1,0:T(8,128)(2,1)S(1)}, bf16[48,16,128]{2,1,0:T(8,128)(2,1)S(1)}, u32[]{:S(2)}, u32[]{:S(2)}) %collective-permute-start.8) | collective-permute-done | bytes 196640 | tf_op jit(solution)/shard_map/ppermute | solution.py:189
  81.7 3.0 %collective-permute-start.9 = (bf16[48,16,128]{2,1,0:T(8,128)(2,1)S(1)}, bf16[48,16,128]{2,1,0:T(8,128)(2,1)S(1)}, u32[]{:S(2)}, u32[]{:S(2)}) collective-permute-start(bf16[48,16,128]{2,1,0:T(8,128)(2,1)S(1)} %add_convert_fusion.7), channel_id=1, source_target_pairs={{0,32},{32,64},{64,96},{96,128},{128,160},{160,192},{192,224},{224... | collective-permute-start | bytes 589832 | tf_op jit(solution)/shard_map/ppermute | solution.py:189
  84.9 1.0 collective-permute-done.16
  85.9 3.0 %collective-permute-start.17 = (bf16[48,16,128]{2,1,0:T(8,128)(2,1)S(1)}, bf16[48,16,128]{2,1,0:T(8,128)(2,1)S(1)}, u32[]{:S(2)}, u32[]{:S(2)}) collective-permute-start(bf16[48,16,128]{2,1,0:T(8,128)(2,1)S(1)} %add_convert_fusion.3), channel_id=1, source_target_pairs={{0,32},{32,64},{64,96},{96,128},{128,160},{160,192},{192,224},{224... | collective-permute-start | bytes 589832 | tf_op jit(solution)/shard_map/ppermute | solution.py:189
  89.1 1.0 collective-permute-done.9
  90.1 3.1 %collective-permute-start.10 = (bf16[48,16,128]{2,1,0:T(8,128)(2,1)S(1)}, bf16[48,16,128]{2,1,0:T(8,128)(2,1)S(1)}, u32[]{:S(2)}, u32[]{:S(2)}) collective-permute-start(bf16[48,16,128]{2,1,0:T(8,128)(2,1)S(1)} %add_convert_fusion.6), channel_id=1, source_target_pairs={{0,32},{32,64},{64,96},{96,128},{128,160},{160,192},{192,224},{224... | collective-permute-start | bytes 589832 | tf_op jit(solution)/shard_map/ppermute | solution.py:189
  93.3 0.9 collective-permute-done.17
  94.3 3.7 %collective-permute-start.18 = (bf16[48,16,128]{2,1,0:T(8,128)(2,1)S(1)}, bf16[48,16,128]{2,1,0:T(8,128)(2,1)S(1)}, u32[]{:S(2)}, u32[]{:S(2)}) collective-permute-start(bf16[48,16,128]{2,1,0:T(8,128)(2,1)S(1)} %add_convert_fusion.2), channel_id=1, source_target_pairs={{0,32},{32,64},{64,96},{96,128},{128,160},{160,192},{192,224},{224... | collective-permute-start | bytes 589832 | tf_op jit(solution)/shard_map/ppermute | solution.py:189
  98.2 2.7 %collective-permute-done.14 = bf16[48,16,128]{2,1,0:T(8,128)(2,1)S(1)} collective-permute-done((bf16[48,16,128]{2,1,0:T(8,128)(2,1)S(1)}, bf16[48,16,128]{2,1,0:T(8,128)(2,1)S(1)}, u32[]{:S(2)}, u32[]{:S(2)}) %collective-permute-start.14) | collective-permute-done | bytes 196640 | tf_op jit(solution)/shard_map/ppermute | solution.py:190
  101.0 0.2 collective-permute-done.18
  101.2 3.8 %collective-permute-done.22 = bf16[48,16,128]{2,1,0:T(8,128)(2,1)S(1)} collective-permute-done((bf16[48,16,128]{2,1,0:T(8,128)(2,1)S(1)}, bf16[48,16,128]{2,1,0:T(8,128)(2,1)S(1)}, u32[]{:S(2)}, u32[]{:S(2)}) %collective-permute-start.22) | collective-permute-done | bytes 196640 | tf_op jit(solution)/shard_map/ppermute | solution.py:190
  105.4 0.3 fusion.4
  105.8 2.4 %fusion.63 = (bf16[2304,160]{0,1:T(8,128)(2,1)S(1)}, f32[2304,160]{0,1:T(8,128)S(1)}) fusion(bf16[2304,1536]{1,0:T(8,128)(2,1)S(1)} %bitcast.64, bf16[1536,160]{0,1:T(8,128)(2,1)S(1)} %bitcast.70), kind=kOutput, calls=%fused_computation.237 | convolution fusion | flops 1132830720 | bytes 9781248 | tf_op jit(solution)/shard_map/dot_general | solution.py:274
  108.7 1.9 %collective-permute-start.29 = (bf16[288,128]{0,1:T(8,128)(2,1)S(1)}, bf16[288,128]{0,1:T(8,128)(2,1)S(1)}, u32[]{:S(2)}, u32[]{:S(2)}) collective-permute-start(bf16[288,128]{0,1:T(8,128)(2,1)S(1)} %get-tuple-element.73), channel_id=1, source_target_pairs={{0,1},{1,2},{2,3},{4,5},{5,6},{6,7},{8,9},{9,10},{10,11},{12,13},{... | collective-permute-start | bytes 221192 | tf_op jit(solution)/shard_map/ppermute | solution.py:19
  110.7 3.6 %collective-permute-start.30 = (bf16[288,128]{0,1:T(8,128)(2,1)S(1)}, bf16[288,128]{0,1:T(8,128)(2,1)S(1)}, u32[]{:S(2)}, u32[]{:S(2)}) collective-permute-start(bf16[288,128]{0,1:T(8,128)(2,1)S(1)} %get-tuple-element.74), channel_id=1, source_target_pairs={{1,0},{2,1},{3,2},{5,4},{6,5},{7,6},{9,8},{10,9},{11,10},{13,12},{... | collective-permute-start | bytes 221192 | tf_op jit(solution)/shard_map/ppermute | solution.py:19
  114.4 0.3 collective-permute-done.29
  114.8 1.8 %collective-permute-done.30 = bf16[288,128]{0,1:T(8,128)(2,1)S(1)} collective-permute-done((bf16[288,128]{0,1:T(8,128)(2,1)S(1)}, bf16[288,128]{0,1:T(8,128)(2,1)S(1)}, u32[]{:S(2)}, u32[]{:S(2)}) %collective-permute-start.30) | collective-permute-done | bytes 73760 | tf_op jit(solution)/shard_map/ppermute | solution.py:19
  116.7 0.2 fusion.57
  117.1 1.9 %collective-permute-start.31 = (bf16[16,48,128]{2,1,0:T(8,128)(2,1)S(1)}, bf16[16,48,128]{2,1,0:T(8,128)(2,1)S(1)}, u32[]{:S(2)}, u32[]{:S(2)}) collective-permute-start(bf16[16,48,128]{2,1,0:T(8,128)(2,1)S(1)} %bitcast.79), channel_id=1, source_target_pairs={{32,0},{64,32},{96,64},{128,96},{160,128},{192,160},{224,192},{33,... | collective-permute-start | bytes 589832 | tf_op jit(solution)/shard_map/ppermute | solution.py:19
  119.2 5.1 %collective-permute-start.32 = (bf16[16,48,128]{2,1,0:T(8,128)(2,1)S(1)}, bf16[16,48,128]{2,1,0:T(8,128)(2,1)S(1)}, u32[]{:S(2)}, u32[]{:S(2)}) collective-permute-start(bf16[16,48,128]{2,1,0:T(8,128)(2,1)S(1)} %bitcast.80), channel_id=1, source_target_pairs={{0,32},{32,64},{64,96},{96,128},{128,160},{160,192},{192,224},{1,3... | collective-permute-start | bytes 589832 | tf_op jit(solution)/shard_map/ppermute | solution.py:19
  124.5 1.3 collective-permute-done.31
  125.9 1.6 %collective-permute-done.32 = bf16[16,48,128]{2,1,0:T(8,128)(2,1)S(1)} collective-permute-done((bf16[16,48,128]{2,1,0:T(8,128)(2,1)S(1)}, bf16[16,48,128]{2,1,0:T(8,128)(2,1)S(1)}, u32[]{:S(2)}, u32[]{:S(2)}) %collective-permute-start.32) | collective-permute-done | bytes 196640 | tf_op jit(solution)/shard_map/ppermute | solution.py:19
  127.6 4.6 %collective-permute-start.33 = (f32[16,16,128]{2,1,0:T(8,128)S(1)}, f32[16,16,128]{2,1,0:T(8,128)S(1)}, u32[]{:S(2)}, u32[]{:S(2)}) collective-permute-start(f32[16,16,128]{2,1,0:T(8,128)S(1)} %get-tuple-element.107), channel_id=1, source_target_pairs={{4,0},{8,4},{12,8},{16,12},{20,16},{24,20},{28,24},{5,1},{9,5},{13... | collective-permute-start | bytes 393224 | tf_op jit(solution)/shard_map/ppermute | solution.py:19
  132.2 2.7 %collective-permute-start.34 = (f32[16,16,128]{2,1,0:T(8,128)S(1)}, f32[16,16,128]{2,1,0:T(8,128)S(1)}, u32[]{:S(2)}, u32[]{:S(2)}) collective-permute-start(f32[16,16,128]{2,1,0:T(8,128)S(1)} %get-tuple-element.108), channel_id=1, source_target_pairs={{0,4},{4,8},{8,12},{12,16},{16,20},{20,24},{24,28},{1,5},{5,9},{9,... | collective-permute-start | bytes 393224 | tf_op jit(solution)/shard_map/ppermute | solution.py:19
  135.0 2.4 %collective-permute-done.33 = f32[16,16,128]{2,1,0:T(8,128)S(1)} collective-permute-done((f32[16,16,128]{2,1,0:T(8,128)S(1)}, f32[16,16,128]{2,1,0:T(8,128)S(1)}, u32[]{:S(2)}, u32[]{:S(2)}) %collective-permute-start.33) | collective-permute-done | bytes 131104 | tf_op jit(solution)/shard_map/ppermute | solution.py:19
  137.4 4.1 %collective-permute-done.34 = f32[16,16,128]{2,1,0:T(8,128)S(1)} collective-permute-done((f32[16,16,128]{2,1,0:T(8,128)S(1)}, f32[16,16,128]{2,1,0:T(8,128)S(1)}, u32[]{:S(2)}, u32[]{:S(2)}) %collective-permute-start.34) | collective-permute-done | bytes 131104 | tf_op jit(solution)/shard_map/ppermute | solution.py:19
  141.5 0.7 fusion.21
  (138 shorter events, 6.5 us)
Async XLA Ops:
  1.9 3.0 %copy-start.4 = (f32[6,3,31]{2,1,0:T(4,128)S(1)}, f32[6,3,31]{2,1,0:T(4,128)}, u32[]{:S(2)}) copy-start(f32[6,3,31]{2,1,0:T(4,128)} %param.8) | copy-start | bytes 6700
  3.6 1.3 copy-start
  4.9 1.7 %copy-start.2 = (f32[16,16,128]{2,1,0:T(8,128)S(1)}, f32[16,16,128]{2,1,0:T(8,128)}, u32[]{:S(2)}) copy-start(f32[16,16,128]{2,1,0:T(8,128)} %param.9) | copy-start | bytes 393220
  6.6 5.0 %copy-start.3 = (s32[6,3072]{1,0:T(8,128)S(1)}, s32[6,3072]{1,0:T(8,128)}, u32[]{:S(2)}) copy-start(s32[6,3072]{1,0:T(8,128)} %param.7) | copy-start | bytes 221188
  6.6 6.8 %copy-start.1 = (bf16[6,48,2,8,128]{4,3,2,1,0:T(8,128)(2,1)S(1)}, bf16[6,48,2,8,128]{4,3,2,1,0:T(8,128)(2,1)}, u32[]{:S(2)}) copy-start(bf16[6,48,2,8,128]{4,3,2,1,0:T(8,128)(2,1)} %param.6) | copy-start | bytes 3538948
  14.7 8.3 %copy-start.5 = (s32[8,40]{1,0:T(8,128)}, s32[8,40]{1,0:T(8,128)S(1)}, u32[]{:S(2)}) copy-start(s32[8,40]{1,0:T(8,128)S(1)} %get-tuple-element.40.late_cell) | copy-start | bytes 3844
  14.7 16.0 %collective-permute-start.23 = (bf16[16,16,128]{2,1,0:T(8,128)(2,1)S(1)}, bf16[16,16,128]{2,1,0:T(8,128)(2,1)S(1)}, u32[]{:S(2)}, u32[]{:S(2)}) collective-permute-start(bf16[16,16,128]{2,1,0:T(8,128)(2,1)S(1)} %convert_element_type.203), channel_id=1, source_target_pairs={{0,4},{4,8},{8,12},{12,16},{16,20},{20,24},{24,28},{1,5},{5,9},{9,... | collective-permute-start | bytes 196616 | tf_op jit(solution)/shard_map/ppermute | solution.py:19
  18.9 11.8 %collective-permute-start.24 = (bf16[16,16,128]{2,1,0:T(8,128)(2,1)S(1)}, bf16[16,16,128]{2,1,0:T(8,128)(2,1)S(1)}, u32[]{:S(2)}, u32[]{:S(2)}) collective-permute-start(bf16[16,16,128]{2,1,0:T(8,128)(2,1)S(1)} %convert_element_type.203), channel_id=1, source_target_pairs={{4,0},{8,4},{12,8},{16,12},{20,16},{24,20},{28,24},{5,1},{9,5},{13... | collective-permute-start | bytes 196616 | tf_op jit(solution)/shard_map/ppermute | solution.py:19
  23.0 39.2 %all-to-all-start = ((bf16[8,56,16,128]{3,2,1,0:T(8,128)(2,1)}), bf16[8,56,16,128]{3,2,1,0:T(8,128)(2,1)S(1)}, u32[]{:S(2)}, u32[]{:S(2)}) async-start(bf16[8,56,16,128]{3,2,1,0:T(8,128)(2,1)} %copy-done), calls=%async_computation | async-start | bytes 3670016 | tf_op jit(solution)/shard_map/all_to_all | solution.py:154
  30.8 8.2 %collective-permute-start.25 = (bf16[16,48,128]{2,1,0:T(8,128)(2,1)S(1)}, bf16[16,48,128]{2,1,0:T(8,128)(2,1)S(1)}, u32[]{:S(2)}, u32[]{:S(2)}) collective-permute-start(bf16[16,48,128]{2,1,0:T(8,128)(2,1)S(1)} %constant_dynamic-update-slice_fusion.7), channel_id=1, source_target_pairs={{0,32},{32,64},{64,96},{96,128},{128,160},{160,192},{192,224},{1,3... | collective-permute-start | bytes 589832 | tf_op jit(solution)/shard_map/ppermute | solution.py:19
  35.8 8.8 %collective-permute-start.26 = (bf16[16,48,128]{2,1,0:T(8,128)(2,1)S(1)}, bf16[16,48,128]{2,1,0:T(8,128)(2,1)S(1)}, u32[]{:S(2)}, u32[]{:S(2)}) collective-permute-start(bf16[16,48,128]{2,1,0:T(8,128)(2,1)S(1)} %constant_dynamic-update-slice_fusion.7), channel_id=1, source_target_pairs={{32,0},{64,32},{96,64},{128,96},{160,128},{192,160},{224,192},{33,... | collective-permute-start | bytes 589832 | tf_op jit(solution)/shard_map/ppermute | solution.py:19
  47.6 7.1 %collective-permute-start.27 = (bf16[288,128]{1,0:T(8,128)(2,1)}, bf16[288,128]{1,0:T(8,128)(2,1)S(1)}, u32[]{:S(2)}, u32[]{:S(2)}) collective-permute-start(bf16[288,128]{1,0:T(8,128)(2,1)} %concatenate.63), channel_id=1, source_target_pairs={{0,1},{1,2},{2,3},{4,5},{5,6},{6,7},{8,9},{9,10},{10,11},{12,13},{... | collective-permute-start | bytes 221192 | tf_op jit(solution)/shard_map/ppermute | solution.py:19
  51.1 5.9 %collective-permute-start.28 = (bf16[288,128]{1,0:T(8,128)(2,1)}, bf16[288,128]{1,0:T(8,128)(2,1)S(1)}, u32[]{:S(2)}, u32[]{:S(2)}) collective-permute-start(bf16[288,128]{1,0:T(8,128)(2,1)} %concatenate.65), channel_id=1, source_target_pairs={{1,0},{2,1},{3,2},{5,4},{6,5},{7,6},{9,8},{10,9},{11,10},{13,12},{... | collective-permute-start | bytes 221192 | tf_op jit(solution)/shard_map/ppermute | solution.py:19
  57.8 4.5 %copy-start.6 = (s32[8,40]{1,0:T(8,128)S(1)}, s32[8,40]{1,0:T(8,128)}, u32[]{:S(2)}) copy-start(s32[8,40]{1,0:T(8,128)} %copy-done.5) | copy-start | bytes 3844
  65.5 8.3 %collective-permute-start.7 = (bf16[24,16,128]{2,1,0:T(8,128)(2,1)S(1)}, bf16[24,16,128]{2,1,0:T(8,128)(2,1)S(1)}, u32[]{:S(2)}, u32[]{:S(2)}) collective-permute-start(bf16[24,16,128]{2,1,0:T(8,128)(2,1)S(1)} %get-tuple-element.47), channel_id=1, source_target_pairs={{0,32},{32,64},{64,96},{96,128},{128,160},{160,192},{192,224},{224... | collective-permute-start | bytes 294920 | tf_op jit(solution)/shard_map/ppermute | solution.py:177
  66.1 10.2 %collective-permute-start.11 = (bf16[24,16,128]{2,1,0:T(8,128)(2,1)S(1)}, bf16[24,16,128]{2,1,0:T(8,128)(2,1)S(1)}, u32[]{:S(2)}, u32[]{:S(2)}) collective-permute-start(bf16[24,16,128]{2,1,0:T(8,128)(2,1)S(1)} %get-tuple-element.51), channel_id=1, source_target_pairs={{32,0},{64,32},{96,64},{128,96},{160,128},{192,160},{224,192},{0,2... | collective-permute-start | bytes 294920 | tf_op jit(solution)/shard_map/ppermute | solution.py:178
  71.6 5.4 %collective-permute-start.15 = (bf16[24,16,128]{2,1,0:T(8,128)(2,1)S(1)}, bf16[24,16,128]{2,1,0:T(8,128)(2,1)S(1)}, u32[]{:S(2)}, u32[]{:S(2)}) collective-permute-start(bf16[24,16,128]{2,1,0:T(8,128)(2,1)S(1)} %get-tuple-element.56), channel_id=1, source_target_pairs={{0,32},{32,64},{64,96},{96,128},{128,160},{160,192},{192,224},{224... | collective-permute-start | bytes 294920 | tf_op jit(solution)/shard_map/ppermute | solution.py:177
  72.8 7.0 %collective-permute-start.19 = (bf16[24,16,128]{2,1,0:T(8,128)(2,1)S(1)}, bf16[24,16,128]{2,1,0:T(8,128)(2,1)S(1)}, u32[]{:S(2)}, u32[]{:S(2)}) collective-permute-start(bf16[24,16,128]{2,1,0:T(8,128)(2,1)S(1)} %get-tuple-element.60), channel_id=1, source_target_pairs={{32,0},{64,32},{96,64},{128,96},{160,128},{192,160},{224,192},{0,2... | collective-permute-start | bytes 294920 | tf_op jit(solution)/shard_map/ppermute | solution.py:178
  73.9 7.7 %collective-permute-start.8 = (bf16[48,16,128]{2,1,0:T(8,128)(2,1)S(1)}, bf16[48,16,128]{2,1,0:T(8,128)(2,1)S(1)}, u32[]{:S(2)}, u32[]{:S(2)}) collective-permute-start(bf16[48,16,128]{2,1,0:T(8,128)(2,1)S(1)} %pad_maximum_fusion.2), channel_id=1, source_target_pairs={{0,32},{32,64},{64,96},{96,128},{128,160},{160,192},{192,224},{224... | collective-permute-start | bytes 589832 | tf_op jit(solution)/shard_map/ppermute | solution.py:189
  76.3 8.4 %collective-permute-start.12 = (bf16[48,16,128]{2,1,0:T(8,128)(2,1)S(1)}, bf16[48,16,128]{2,1,0:T(8,128)(2,1)S(1)}, u32[]{:S(2)}, u32[]{:S(2)}) collective-permute-start(bf16[48,16,128]{2,1,0:T(8,128)(2,1)S(1)} %pad_maximum_fusion.3), channel_id=1, source_target_pairs={{32,0},{64,32},{96,64},{128,96},{160,128},{192,160},{224,192},{0,2... | collective-permute-start | bytes 589832 | tf_op jit(solution)/shard_map/ppermute | solution.py:190
  77.1 28.7 %slice-start = ((s8[7077888]{0:T(1024)(128)(4,1)}), s8[4194304]{0:T(1024)(128)(4,1)S(1)}, s32[]{:S(2)}) async-start(s8[7077888]{0:T(1024)(128)(4,1)} %bitcast.62), calls=%async_computation.1 | async-start | bytes 8388608
  77.1 8.7 %collective-permute-start.16 = (bf16[48,16,128]{2,1,0:T(8,128)(2,1)S(1)}, bf16[48,16,128]{2,1,0:T(8,128)(2,1)S(1)}, u32[]{:S(2)}, u32[]{:S(2)}) collective-permute-start(bf16[48,16,128]{2,1,0:T(8,128)(2,1)S(1)} %pad_maximum_fusion.4), channel_id=1, source_target_pairs={{0,32},{32,64},{64,96},{96,128},{128,160},{160,192},{192,224},{224... | collective-permute-start | bytes 589832 | tf_op jit(solution)/shard_map/ppermute | solution.py:189
  79.9 9.0 %collective-permute-start.20 = (bf16[48,16,128]{2,1,0:T(8,128)(2,1)S(1)}, bf16[48,16,128]{2,1,0:T(8,128)(2,1)S(1)}, u32[]{:S(2)}, u32[]{:S(2)}) collective-permute-start(bf16[48,16,128]{2,1,0:T(8,128)(2,1)S(1)} %pad_maximum_fusion.5), channel_id=1, source_target_pairs={{32,0},{64,32},{96,64},{128,96},{160,128},{192,160},{224,192},{0,2... | collective-permute-start | bytes 589832 | tf_op jit(solution)/shard_map/ppermute | solution.py:190
  81.7 8.4 %collective-permute-start.9 = (bf16[48,16,128]{2,1,0:T(8,128)(2,1)S(1)}, bf16[48,16,128]{2,1,0:T(8,128)(2,1)S(1)}, u32[]{:S(2)}, u32[]{:S(2)}) collective-permute-start(bf16[48,16,128]{2,1,0:T(8,128)(2,1)S(1)} %add_convert_fusion.7), channel_id=1, source_target_pairs={{0,32},{32,64},{64,96},{96,128},{128,160},{160,192},{192,224},{224... | collective-permute-start | bytes 589832 | tf_op jit(solution)/shard_map/ppermute | solution.py:189
  84.8 8.4 %collective-permute-start.13 = (bf16[48,16,128]{2,1,0:T(8,128)(2,1)S(1)}, bf16[48,16,128]{2,1,0:T(8,128)(2,1)S(1)}, u32[]{:S(2)}, u32[]{:S(2)}) collective-permute-start(bf16[48,16,128]{2,1,0:T(8,128)(2,1)S(1)} %add_convert_fusion.5), channel_id=1, source_target_pairs={{32,0},{64,32},{96,64},{128,96},{160,128},{192,160},{224,192},{0,2... | collective-permute-start | bytes 589832 | tf_op jit(solution)/shard_map/ppermute | solution.py:190
  85.9 8.4 %collective-permute-start.17 = (bf16[48,16,128]{2,1,0:T(8,128)(2,1)S(1)}, bf16[48,16,128]{2,1,0:T(8,128)(2,1)S(1)}, u32[]{:S(2)}, u32[]{:S(2)}) collective-permute-start(bf16[48,16,128]{2,1,0:T(8,128)(2,1)S(1)} %add_convert_fusion.3), channel_id=1, source_target_pairs={{0,32},{32,64},{64,96},{96,128},{128,160},{160,192},{192,224},{224... | collective-permute-start | bytes 589832 | tf_op jit(solution)/shard_map/ppermute | solution.py:189
  89.0 9.1 %collective-permute-start.21 = (bf16[48,16,128]{2,1,0:T(8,128)(2,1)S(1)}, bf16[48,16,128]{2,1,0:T(8,128)(2,1)S(1)}, u32[]{:S(2)}, u32[]{:S(2)}) collective-permute-start(bf16[48,16,128]{2,1,0:T(8,128)(2,1)S(1)} %add_convert_fusion.1), channel_id=1, source_target_pairs={{32,0},{64,32},{96,64},{128,96},{160,128},{192,160},{224,192},{0,2... | collective-permute-start | bytes 589832 | tf_op jit(solution)/shard_map/ppermute | solution.py:190
  90.1 8.1 %collective-permute-start.10 = (bf16[48,16,128]{2,1,0:T(8,128)(2,1)S(1)}, bf16[48,16,128]{2,1,0:T(8,128)(2,1)S(1)}, u32[]{:S(2)}, u32[]{:S(2)}) collective-permute-start(bf16[48,16,128]{2,1,0:T(8,128)(2,1)S(1)} %add_convert_fusion.6), channel_id=1, source_target_pairs={{0,32},{32,64},{64,96},{96,128},{128,160},{160,192},{192,224},{224... | collective-permute-start | bytes 589832 | tf_op jit(solution)/shard_map/ppermute | solution.py:189
  93.2 7.7 %collective-permute-start.14 = (bf16[48,16,128]{2,1,0:T(8,128)(2,1)S(1)}, bf16[48,16,128]{2,1,0:T(8,128)(2,1)S(1)}, u32[]{:S(2)}, u32[]{:S(2)}) collective-permute-start(bf16[48,16,128]{2,1,0:T(8,128)(2,1)S(1)} %add_convert_fusion.4), channel_id=1, source_target_pairs={{32,0},{64,32},{96,64},{128,96},{160,128},{192,160},{224,192},{0,2... | collective-permute-start | bytes 589832 | tf_op jit(solution)/shard_map/ppermute | solution.py:190
  94.3 6.9 %collective-permute-start.18 = (bf16[48,16,128]{2,1,0:T(8,128)(2,1)S(1)}, bf16[48,16,128]{2,1,0:T(8,128)(2,1)S(1)}, u32[]{:S(2)}, u32[]{:S(2)}) collective-permute-start(bf16[48,16,128]{2,1,0:T(8,128)(2,1)S(1)} %add_convert_fusion.2), channel_id=1, source_target_pairs={{0,32},{32,64},{64,96},{96,128},{128,160},{160,192},{192,224},{224... | collective-permute-start | bytes 589832 | tf_op jit(solution)/shard_map/ppermute | solution.py:189
  98.1 7.0 %collective-permute-start.22 = (bf16[48,16,128]{2,1,0:T(8,128)(2,1)S(1)}, bf16[48,16,128]{2,1,0:T(8,128)(2,1)S(1)}, u32[]{:S(2)}, u32[]{:S(2)}) collective-permute-start(bf16[48,16,128]{2,1,0:T(8,128)(2,1)S(1)} %add_convert_fusion), channel_id=1, source_target_pairs={{32,0},{64,32},{96,64},{128,96},{160,128},{192,160},{224,192},{0,2... | collective-permute-start | bytes 589832 | tf_op jit(solution)/shard_map/ppermute | solution.py:190
  100.9 4.8 %slice-start.1 = ((s8[7077888]{0:T(1024)(128)(4,1)}), s8[2883584]{0:T(1024)(128)(4,1)S(1)}, s32[]{:S(2)}) async-start(s8[7077888]{0:T(1024)(128)(4,1)} %bitcast.62), calls=%async_computation.2 | async-start | bytes 5767168
  108.7 5.9 %collective-permute-start.29 = (bf16[288,128]{0,1:T(8,128)(2,1)S(1)}, bf16[288,128]{0,1:T(8,128)(2,1)S(1)}, u32[]{:S(2)}, u32[]{:S(2)}) collective-permute-start(bf16[288,128]{0,1:T(8,128)(2,1)S(1)} %get-tuple-element.73), channel_id=1, source_target_pairs={{0,1},{1,2},{2,3},{4,5},{5,6},{6,7},{8,9},{9,10},{10,11},{12,13},{... | collective-permute-start | bytes 221192 | tf_op jit(solution)/shard_map/ppermute | solution.py:19
  110.7 5.8 %collective-permute-start.30 = (bf16[288,128]{0,1:T(8,128)(2,1)S(1)}, bf16[288,128]{0,1:T(8,128)(2,1)S(1)}, u32[]{:S(2)}, u32[]{:S(2)}) collective-permute-start(bf16[288,128]{0,1:T(8,128)(2,1)S(1)} %get-tuple-element.74), channel_id=1, source_target_pairs={{1,0},{2,1},{3,2},{5,4},{6,5},{7,6},{9,8},{10,9},{11,10},{13,12},{... | collective-permute-start | bytes 221192 | tf_op jit(solution)/shard_map/ppermute | solution.py:19
  117.1 8.8 %collective-permute-start.31 = (bf16[16,48,128]{2,1,0:T(8,128)(2,1)S(1)}, bf16[16,48,128]{2,1,0:T(8,128)(2,1)S(1)}, u32[]{:S(2)}, u32[]{:S(2)}) collective-permute-start(bf16[16,48,128]{2,1,0:T(8,128)(2,1)S(1)} %bitcast.79), channel_id=1, source_target_pairs={{32,0},{64,32},{96,64},{128,96},{160,128},{192,160},{224,192},{33,... | collective-permute-start | bytes 589832 | tf_op jit(solution)/shard_map/ppermute | solution.py:19
  119.2 8.3 %collective-permute-start.32 = (bf16[16,48,128]{2,1,0:T(8,128)(2,1)S(1)}, bf16[16,48,128]{2,1,0:T(8,128)(2,1)S(1)}, u32[]{:S(2)}, u32[]{:S(2)}) collective-permute-start(bf16[16,48,128]{2,1,0:T(8,128)(2,1)S(1)} %bitcast.80), channel_id=1, source_target_pairs={{0,32},{32,64},{64,96},{96,128},{128,160},{160,192},{192,224},{1,3... | collective-permute-start | bytes 589832 | tf_op jit(solution)/shard_map/ppermute | solution.py:19
  127.6 9.8 %collective-permute-start.33 = (f32[16,16,128]{2,1,0:T(8,128)S(1)}, f32[16,16,128]{2,1,0:T(8,128)S(1)}, u32[]{:S(2)}, u32[]{:S(2)}) collective-permute-start(f32[16,16,128]{2,1,0:T(8,128)S(1)} %get-tuple-element.107), channel_id=1, source_target_pairs={{4,0},{8,4},{12,8},{16,12},{20,16},{24,20},{28,24},{5,1},{9,5},{13... | collective-permute-start | bytes 393224 | tf_op jit(solution)/shard_map/ppermute | solution.py:19
  132.2 9.3 %collective-permute-start.34 = (f32[16,16,128]{2,1,0:T(8,128)S(1)}, f32[16,16,128]{2,1,0:T(8,128)S(1)}, u32[]{:S(2)}, u32[]{:S(2)}) collective-permute-start(f32[16,16,128]{2,1,0:T(8,128)S(1)} %get-tuple-element.108), channel_id=1, source_target_pairs={{0,4},{4,8},{8,12},{12,16},{16,20},{20,24},{24,28},{1,5},{5,9},{9,... | collective-permute-start | bytes 393224 | tf_op jit(solution)/shard_map/ppermute | solution.py:19
